TPU v7x, 256 devices: a whole 4x4x8 slice. The times are simulated.
256 devices in a mesh: seq: 32 (over z_lo, y, x), head: 8 (over z_hi, core).
Axes of the slice: x: 4, y: 4, z: 8 (z_hi: 4, z_lo: 2; z = z_hi * 2 + z_lo), core: 2. Of those that a mesh axis runs over, the one named last changes fastest.
Arguments:
- queries: bfloat16 [32768, 1024], P(('seq', 'head')), may hold values from -10 to 10, as said below
- keys: bfloat16 [32768, 1024], P(('seq', 'head')), may hold values from -8 to 8, as said below
- values: bfloat16 [32768, 1024], P(('seq', 'head')), may hold values from -6 to 6
- grad_out: bfloat16 [32768, 1024], P(('seq', 'head')), may hold values from -6 to 6
- doc_ids: int32 [32768], replicated, may hold values from 0 to 2, never falling along the last dimension, each value on 1 to 16384 neighbouring positions
Outputs:
- attended: bfloat16 [32768, 1024], P(('seq', 'head'))
- grad_queries: bfloat16 [32768, 1024], P(('seq', 'head'))
- grad_keys: bfloat16 [32768, 1024], P(('seq', 'head'))
- grad_values: bfloat16 [32768, 1024], P(('seq', 'head'))
Inputs may be any that keep to these rules, and one draw needn't show every extreme that they name: `queries`: Real-valued entries. `keys`: Real-valued entries. `doc_ids`: document ids never fall along the sequence; the longest document holds exactly half of the 32768 tokens.
All inputs are finite; a program needn't handle non-finite values.
Results may differ from a plain program's by a relative error of at most 0.011.
Values may be sent and summed in bfloat16 or wider, within the bound.
A program may use at most 128 MiB of HBM per device.

v0:
```python
import jax
import jax.numpy as jnp
from jax import lax
from jax.experimental import pallas as pl
from jax.experimental.pallas import tpu as pltpu
from jax.sharding import PartitionSpec as P

F32 = jnp.float32
BF16 = jnp.bfloat16
I32 = jnp.int32
BIG = 1e30
NH = 8
NB = 128
MESH = pl.DeviceIdType.MESH


def iota(shape, dim):
    return lax.broadcasted_iota(I32, shape, dim)


def token_of(parity, w, h):
    t, u, a = (w >> 4) & 3, (w >> 2) & 3, w & 3
    return a * 32 + parity + 2 * ((h + t) & 3) + 8 * ((h // 4 + u) & 3)


def nn(a, b):
    return lax.dot_general(a, b, (((1,), (0,)), ((), ())), preferred_element_type=F32)


def attend_kernel(
    q_ref, k_ref, v_ref, do_ref, docs_ref, out_ref,
    send, inbuf, kv2, kv8, kv32, KX, KT, VT, VN, QG, QXT, QXT32, QM, DOM, DOT,
    ST, OT, DQT, ACC, g2, r2, g8, r8, g32, r32, g32z, r32z, og,
    in_ss, in_rs, loc_s, l2_ss, l2_rs, l8_ss, l8_rs, l32_ss, l32_rs, z_ss, z_rs, out_ss, out_rs,
):
    h = lax.axis_index("head")
    s = lax.axis_index("seq")
    pair = s + 1 - 2 * (s % 2)
    base8 = (s // 8) * 8
    base16 = (s // 16) * 16
    zpeer = (s + 16) % 32

    def plane_peer(k):
        return base16 + (s - base16 + k) % 16

    def oct_peer(k):
        return base8 + (s - base8 + k) % 8

    def head_peer(k):
        return (h + k) % NH

    barrier = pltpu.get_barrier_semaphore()
    for k in range(1, NH):
        pl.semaphore_signal(barrier, inc=1, device_id={"head": head_peer(k)}, device_id_type=MESH)
    for k in range(1, 16):
        pl.semaphore_signal(barrier, inc=1, device_id={"seq": plane_peer(k)}, device_id_type=MESH)
    pl.semaphore_signal(barrier, inc=1, device_id={"seq": zpeer}, device_id_type=MESH)

    lane = iota((64, 128), 1)
    low64 = lane < 64

    def permute_two(first, a_ref, b_ref):
        for g in range(NH):
            rho = iota((NB, NB), 0)
            mat = (iota((NB, NB), 1) == token_of(rho >> 6, rho & 63, g)).astype(F32).astype(BF16)
            cols = slice(g * 128, g * 128 + 128)
            both = jnp.concatenate([a_ref[:, cols], b_ref[:, cols]], axis=1)
            res = nn(mat, both)
            for i in range(2):
                even, odd = res[0:64, i * 128:i * 128 + 128], res[64:128, i * 128:i * 128 + 128]
                send[first + i, g, 0:64] = jnp.where(low64, even, odd).astype(BF16)
                send[first + i, g, 64:128] = jnp.where(low64, odd, even).astype(BF16)

    def in_copy(t, k):
        return pltpu.make_async_remote_copy(
            src_ref=send.at[t, head_peer(k)], dst_ref=inbuf.at[t, h],
            send_sem=in_ss.at[t * 7 + k - 1], recv_sem=in_rs.at[t * 7 + k - 1],
            device_id={"head": head_peer(k)}, device_id_type=MESH)

    def in_local(t):
        return pltpu.make_async_copy(send.at[t, h], inbuf.at[t, h], loc_s.at[t])

    def start_in(t):
        for k in range(1, NH):
            in_copy(t, k).start()
        in_local(t).start()

    def wait_in(t):
        for k in range(1, NH):
            in_copy(t, k).wait_recv()
        in_local(t).wait()

    permute_two(0, k_ref, v_ref)
    pl.semaphore_wait(barrier, 23)
    start_in(0)
    start_in(1)
    permute_two(2, q_ref, do_ref)
    start_in(2)
    start_in(3)

    docs = docs_ref[...]

    def count(limit):
        c = jnp.sum((docs < limit).astype(F32), axis=0, keepdims=True)
        return jnp.sum(c, axis=1, keepdims=True).astype(I32)

    bound1, bound2 = count(1), count(2)

    def doc_of(pos):
        return (pos >= bound1).astype(I32) + (pos >= bound2).astype(I32)

    lane128 = iota((128, 128), 1)
    row128 = iota((128, 128), 0)
    half = [lane128 < 64, lane128 >= 64]
    feat_lane = [lane128 - 64, lane128]
    half_row = [row128 < 64, row128 >= 64]
    feat_row = [row128 - 64, row128]

    def key_place(level, c):
        r = row128 + c * 128
        if level == 0:
            return s, r >> 7, r & 127
        if level == 1:
            return jnp.where((r >> 9) == 0, s, pair), (r >> 6) & 7, r & 63
        if level == 2:
            return base8 + ((s + (r >> 7)) & 7), (r >> 4) & 7, r & 15
        plane = jnp.where(((r >> 5) & 1) == 0, base16, 16 - base16)
        return plane + ((s + (r >> 6)) & 15), (r >> 2) & 7, r & 3

    def fill_features(c, carry):
        for level in range(4):
            seqs, src, w = key_place(level, c)
            start = seqs * 1024 + src * 128
            for j in range(2):
                parity = j ^ (w >> 6)
                doc = doc_of(start + token_of(parity, w & 63, h))
                hot = (feat_lane[j] == doc) | (feat_lane[j] == 3)
                KX[level, j, pl.ds(c * 128, 128)] = jnp.where(hot, 1.0, 0.0).astype(BF16)
        return carry

    lax.fori_loop(0, 8, fill_features, 0)

    for c in range(8):
        if c == 0:
            src, w = lane128 >> 4, lane128 & 15
        elif c < 4:
            i = lane128 + (c - 1) * 128
            src = (i * 1366) >> 16
            w = 16 + i - src * 48
        else:
            i = lane128 + (c - 4) * 128
            src, w = i >> 6, 64 + (i & 63)
        for j in range(2):
            parity = j ^ (w >> 6)
            doc = doc_of(s * 1024 + src * 128 + token_of(parity, w & 63, h))
            hide = (feat_row[j] >= 0) & (feat_row[j] < 3) & (feat_row[j] != doc)
            QXT[j, c] = jnp.where(hide, -BIG, 0.0).astype(BF16)
            if c == 0:
                hide = hide | ((feat_row[j] == 3) & (w >= 4))
                QXT32[j] = jnp.where(hide, -BIG, 0.0).astype(BF16)

    ACC[...] = jnp.zeros(ACC.shape, F32)

    wait_in(0)
    wait_in(1)
    l2_copy = pltpu.make_async_remote_copy(
        src_ref=inbuf.at[pl.ds(0, 2), :, pl.ds(0, 64), :], dst_ref=kv2.at[1],
        send_sem=l2_ss.at[0], recv_sem=l2_rs.at[0], device_id={"seq": pair}, device_id_type=MESH)
    l2_copy.start()

    pick_row, pick_col = iota((32, 128), 0), iota((32, 128), 1)
    pick = (pick_col == (pick_row >> 2) * 16 + (pick_row & 3)).astype(F32).astype(BF16)
    for t in range(2):
        kv32[0, 0, t] = nn(pick, inbuf[t, :, 0:16].reshape(128, 128)).astype(BF16)
    z_copy = pltpu.make_async_remote_copy(
        src_ref=kv32.at[0, 0], dst_ref=kv32.at[0, 1],
        send_sem=z_ss.at[0], recv_sem=z_rs.at[0], device_id={"seq": zpeer}, device_id_type=MESH)
    z_copy.start()

    def l8_copy(k):
        return pltpu.make_async_remote_copy(
            src_ref=inbuf.at[pl.ds(0, 2), :, pl.ds(0, 16), :], dst_ref=kv8.at[8 - k],
            send_sem=l8_ss.at[k - 1], recv_sem=l8_rs.at[k - 1], device_id={"seq": oct_peer(k)}, device_id_type=MESH)

    for k in range(1, 8):
        l8_copy(k).start()
    for t in range(2):
        kv2[0, t] = inbuf[t, :, 0:64]
        kv8[0, t] = inbuf[t, :, 0:16]

    def l32_copy(k):
        return pltpu.make_async_remote_copy(
            src_ref=kv32.at[0], dst_ref=kv32.at[16 - k],
            send_sem=l32_ss.at[k - 1], recv_sem=l32_rs.at[k - 1], device_id={"seq": plane_peer(k)}, device_id_type=MESH)

    def prepare(level, load):
        def chunk(c, carry):
            rows = pl.ds(pl.multiple_of(c * 128, 128), 128)
            key = load(0, c).astype(F32)
            val = load(1, c)
            for j in range(2):
                KX[level, j, rows] = jnp.where(half[j], key, KX[level, j, rows].astype(F32)).astype(BF16)
            KT[level, :, rows] = key.T.astype(BF16)
            VT[level, :, rows] = val.astype(F32).T.astype(BF16)
            VN[level, rows] = val
            return carry

        lax.fori_loop(0, 8, chunk, 0)

    prepare(0, lambda t, c: inbuf[t, c])

    z_copy.wait()
    for k in range(1, 16):
        l32_copy(k).start()

    def gather_order(t):
        x = inbuf.at[t]
        QG[0:128] = x[:, 0:16].reshape(128, 128)
        QG[128:512] = x[:, 16:64].reshape(384, 128)
        QG[512:1024] = x[:, 64:128].reshape(512, 128)

    wait_in(2)
    gather_order(2)
    for c in range(8):
        x = QG[c * 128:c * 128 + 128].astype(F32) * 0.125
        xt = x.T
        for j in range(2):
            QM[j, c * 128:c * 128 + 128] = jnp.where(half[j], x, 0.0).astype(BF16)
            QXT[j, c] = jnp.where(half_row[j], xt, QXT[j, c].astype(F32)).astype(BF16)
            if c == 0:
                QXT32[j] = jnp.where(half_row[j], xt, QXT32[j].astype(F32)).astype(BF16)

    def wide(ref, j, b):
        return jnp.concatenate([ref[j, 2 * b], ref[j, 2 * b + 1]], axis=1)

    def forward(level, j, qxt):
        sc = nn(KX[level, j], qxt)
        m = jnp.max(sc, axis=0, keepdims=True)
        w = jnp.exp(sc - m)
        total = jnp.sum(w, axis=0, keepdims=True)
        o = nn(VT[level, 64 * j:64 * j + 64], w.astype(BF16))
        return m, total, o

    def merge(j, b, width, m, total, o):
        m0, l0, o0 = ST[0, j, b, :, :width], ST[1, j, b, :, :width], OT[j, b, :, :width]
        mm = jnp.maximum(m0, m)
        e0, e1 = jnp.exp(m0 - mm), jnp.exp(m - mm)
        ST[0, j, b, :, :width] = mm
        ST[1, j, b, :, :width] = l0 * e0 + total * e1
        OT[j, b, :, :width] = o0 * e0 + o * e1

    def forward_first(b, carry):
        for j in range(2):
            m, total, o = forward(0, j, wide(QXT, j, b))
            ST[0, j, b] = m
            ST[1, j, b] = total
            OT[j, b] = o
        return carry

    lax.fori_loop(0, 4, forward_first, 0)

    l2_copy.wait()
    prepare(1, lambda t, c: kv2[c // 4, t, pl.ds((c % 4) * 2, 2)].reshape(128, 128))

    def forward_second(b, carry):
        for j in range(2):
            merge(j, b, 256, *forward(1, j, wide(QXT, j, b)))
        return carry

    lax.fori_loop(0, 2, forward_second, 0)

    for k in range(1, 8):
        l8_copy(k).wait()
    prepare(2, lambda t, c: kv8[c, t].reshape(128, 128))
    for j in range(2):
        merge(j, 0, 128, *forward(2, j, QXT[j, 0]))
    for k in range(1, 16):
        l32_copy(k).wait()
    prepare(3, lambda t, c: kv32[pl.ds(2 * c, 2), :, t].reshape(128, 128))
    for j in range(2):
        merge(j, 0, 128, *forward(3, j, QXT32[j]))

    wait_in(3)
    gather_order(3)
    for c in range(8):
        x = QG[c * 128:c * 128 + 128].astype(F32)
        xt = x.T
        for j in range(2):
            DOM[j, c * 128:c * 128 + 128] = jnp.where(half[j], x, 0.0).astype(BF16)
            DOT[j, c] = jnp.where(half_row[j], xt, 0.0).astype(BF16)

    def out_copy(t, k):
        return pltpu.make_async_remote_copy(
            src_ref=og.at[t, head_peer(k)], dst_ref=out_ref.at[t, h],
            send_sem=out_ss.at[t * 7 + k - 1], recv_sem=out_rs.at[t * 7 + k - 1],
            device_id={"head": head_peer(k)}, device_id_type=MESH)

    def out_local(t):
        return pltpu.make_async_copy(og.at[t, h], out_ref.at[t, h], loc_s.at[t])

    def start_out(t):
        for k in range(1, NH):
            out_copy(t, k).start()
        out_local(t).start()

    def scatter_order(t):
        og[t, :, 0:16] = QG[0:128].reshape(8, 16, 128)
        og[t, :, 16:64] = QG[128:512].reshape(8, 48, 128)
        og[t, :, 64:128] = QG[512:1024].reshape(8, 64, 128)

    for b in range(4):
        outs = []
        for j in range(2):
            total = ST[1, j, b]
            o = OT[j, b] / total
            outs.append(o)
            dot_up = wide(DOT, j, b)[64 * j:64 * j + 64].astype(F32)
            ST[0, j, b] = ST[0, j, b] + jnp.log(total)
            ST[1, j, b] = jnp.sum(dot_up * o, axis=0, keepdims=True)
        QG[b * 256:b * 256 + 256] = jnp.concatenate(outs, axis=0).T.astype(BF16)
    scatter_order(0)
    start_out(0)

    def backward(level, j, b, width, qxt, dot_t, rows):
        p = jnp.exp(nn(KX[level, j], qxt) - ST[0, j, b, :, :width])
        ACC[level, 1] += nn(p.astype(BF16), DOM[j, rows])
        dp = nn(VN[level], dot_t)
        ds = (p * (dp - ST[1, j, b, :, :width])).astype(BF16)
        ACC[level, 0] += nn(ds, QM[j, rows])
        return nn(KT[level, 64 * j:64 * j + 64], ds)

    DQT[...] = jnp.zeros(DQT.shape, F32)
    for j in range(2):
        DQT[j, 0, :, 0:128] += backward(3, j, 0, 128, QXT32[j], DOT[j, 0], pl.ds(0, 128))
    for t in range(2):
        g32[:, :, t] = ACC[3, t].reshape(16, 2, 32, 128).astype(BF16)

    def g32_copy(k):
        return pltpu.make_async_remote_copy(
            src_ref=g32.at[k], dst_ref=r32.at[16 - k],
            send_sem=l32_ss.at[14 + k], recv_sem=l32_rs.at[14 + k],
            device_id={"seq": plane_peer(k)}, device_id_type=MESH)

    for k in range(1, 16):
        g32_copy(k).start()

    for j in range(2):
        DQT[j, 0, :, 0:128] += backward(2, j, 0, 128, QXT[j, 0], DOT[j, 0], pl.ds(0, 128))
    for t in range(2):
        g8[:, t] = ACC[2, t].reshape(8, 128, 128).astype(BF16)

    def g8_copy(k):
        return pltpu.make_async_remote_copy(
            src_ref=g8.at[k], dst_ref=r8.at[8 - k],
            send_sem=l8_ss.at[6 + k], recv_sem=l8_rs.at[6 + k],
            device_id={"seq": oct_peer(k)}, device_id_type=MESH)

    for k in range(1, 8):
        g8_copy(k).start()

    def backward_level(level):
        def body(b, carry):
            for j in range(2):
                rows = pl.ds(pl.multiple_of(b * 256, 256), 256)
                DQT[j, b] += backward(level, j, b, 256, wide(QXT, j, b), wide(DOT, j, b), rows)
            return carry

        return body

    lax.fori_loop(0, 2, backward_level(1), 0)
    for t in range(2):
        g2[t] = ACC[1, t, 512:1024].reshape(8, 64, 128).astype(BF16)
    g2_copy = pltpu.make_async_remote_copy(
        src_ref=g2, dst_ref=r2, send_sem=l2_ss.at[1], recv_sem=l2_rs.at[1],
        device_id={"seq": pair}, device_id_type=MESH)
    g2_copy.start()

    for k in range(1, 16):
        g32_copy(k).wait()
    sum32 = []
    for t in range(2):
        mine, theirs = ACC[3, t, 0:32], ACC[3, t, 32:64]
        for m in range(1, 16):
            mine += r32[m, 0, t].astype(F32)
            theirs += r32[m, 1, t].astype(F32)
        ACC[3, t, 0:32] = mine
        g32z[t] = theirs.astype(BF16)
    gz_copy = pltpu.make_async_remote_copy(
        src_ref=g32z, dst_ref=r32z, send_sem=z_ss.at[1], recv_sem=z_rs.at[1],
        device_id={"seq": zpeer}, device_id_type=MESH)
    gz_copy.start()

    lax.fori_loop(0, 4, backward_level(0), 0)

    for b in range(4):
        both = jnp.concatenate([DQT[0, b], DQT[1, b]], axis=0) * 0.125
        QG[b * 256:b * 256 + 256] = both.T.astype(BF16)
    scatter_order(1)
    start_out(1)

    g2_copy.wait()
    for k in range(1, 8):
        g8_copy(k).wait()
    gz_copy.wait()
    put_row, put_col = iota((128, 32), 0), iota((128, 32), 1)
    put = (put_row == (put_col >> 2) * 16 + (put_col & 3)).astype(F32).astype(BF16)
    for t in range(2):
        acc1 = ACC.at[0, t]
        t8 = ACC[2, t, 0:128]
        for m in range(1, 8):
            t8 += r8[m, t].astype(F32)
        t32 = ACC[3, t, 0:32] + r32z[t].astype(F32)
        hi = t32.astype(BF16)
        lo = (t32 - hi.astype(F32)).astype(BF16)
        t8 = t8 + nn(put, hi) + nn(put, lo)
        for b in range(8):
            t2 = ACC[1, t, b * 64:b * 64 + 64] + r2[t, b].astype(F32)
            own = acc1[b * 128:b * 128 + 128]
            og[2 + t, b, 0:16] = (own[0:16] + t2[0:16] + t8[b * 16:b * 16 + 16]).astype(BF16)
            og[2 + t, b, 16:64] = (own[16:64] + t2[16:64]).astype(BF16)
            og[2 + t, b, 64:128] = own[64:128].astype(BF16)
        start_out(2 + t)

    for t in range(4):
        for k in range(1, NH):
            in_copy(t, k).wait_send()
    for t in range(4):
        for k in range(1, NH):
            out_copy(t, k).wait()
        out_local(t).wait()


def restore_kernel(packed_ref, a_ref, q_ref, k_ref, v_ref):
    low64 = iota((64, 128), 1) < 64
    outs = (a_ref, q_ref, k_ref, v_ref)
    for g in range(NH):
        rho = iota((NB, NB), 1)
        mat = (iota((NB, NB), 0) == token_of(rho >> 6, rho & 63, g)).astype(F32).astype(BF16)
        cols = []
        for t in range(4):
            first, second = packed_ref[t, g, 0:64].astype(F32), packed_ref[t, g, 64:128].astype(F32)
            cols.append(jnp.concatenate(
                [jnp.where(low64, first, second), jnp.where(low64, second, first)], axis=0).astype(BF16))
        res = nn(mat, jnp.concatenate(cols, axis=1))
        for t in range(4):
            outs[t][:, g * 128:g * 128 + 128] = res[:, t * 128:t * 128 + 128].astype(BF16)


def body(queries, keys, values, grad_out, doc_ids):
    vmem = pl.BlockSpec(memory_space=pltpu.VMEM)
    dma = pltpu.SemaphoreType.DMA
    packed = pl.pallas_call(
        attend_kernel,
        out_shape=jax.ShapeDtypeStruct((4, NH, NB, 128), BF16),
        in_specs=[vmem] * 5,
        out_specs=vmem,
        scratch_shapes=[
            pltpu.VMEM((4, NH, NB, 128), BF16),
            pltpu.VMEM((4, NH, NB, 128), BF16),
            pltpu.VMEM((2, 2, 8, 64, 128), BF16),
            pltpu.VMEM((8, 2, 8, 16, 128), BF16),
            pltpu.VMEM((16, 2, 2, 32, 128), BF16),
            pltpu.VMEM((4, 2, 1024, 128), BF16),
            pltpu.VMEM((4, 128, 1024), BF16),
            pltpu.VMEM((4, 128, 1024), BF16),
            pltpu.VMEM((4, 1024, 128), BF16),
            pltpu.VMEM((1024, 128), BF16),
            pltpu.VMEM((2, 8, 128, 128), BF16),
            pltpu.VMEM((2, 128, 128), BF16),
            pltpu.VMEM((2, 1024, 128), BF16),
            pltpu.VMEM((2, 1024, 128), BF16),
            pltpu.VMEM((2, 8, 128, 128), BF16),
            pltpu.VMEM((2, 2, 4, 1, 256), F32),
            pltpu.VMEM((2, 4, 64, 256), F32),
            pltpu.VMEM((2, 4, 64, 256), F32),
            pltpu.VMEM((4, 2, 1024, 128), F32),
            pltpu.VMEM((2, 8, 64, 128), BF16),
            pltpu.VMEM((2, 8, 64, 128), BF16),
            pltpu.VMEM((8, 2, 128, 128), BF16),
            pltpu.VMEM((8, 2, 128, 128), BF16),
            pltpu.VMEM((16, 2, 2, 32, 128), BF16),
            pltpu.VMEM((16, 2, 2, 32, 128), BF16),
            pltpu.VMEM((2, 32, 128), BF16),
            pltpu.VMEM((2, 32, 128), BF16),
            pltpu.VMEM((4, NH, NB, 128), BF16),
            dma((28,)), dma((28,)), dma((4,)),
            dma((2,)), dma((2,)), dma((14,)), dma((14,)), dma((30,)), dma((30,)),
            dma((2,)), dma((2,)), dma((28,)), dma((28,)),
        ],
        compiler_params=pltpu.CompilerParams(
            collective_id=0, has_side_effects=True, vmem_limit_bytes=56 * 1024 * 1024),
        name="attend",
    )(queries, keys, values, grad_out, doc_ids.reshape(256, 128))
    shape = jax.ShapeDtypeStruct(queries.shape, BF16)
    return pl.pallas_call(
        restore_kernel,
        out_shape=(shape, shape, shape, shape),
        in_specs=[vmem],
        out_specs=(vmem, vmem, vmem, vmem),
        compiler_params=pltpu.CompilerParams(vmem_limit_bytes=32 * 1024 * 1024),
        name="restore",
    )(packed)


def solution(mesh):
    spec = P(("seq", "head"), None)
    return jax.shard_map(
        body, mesh=mesh, in_specs=(spec, spec, spec, spec, P()), out_specs=(spec, spec, spec, spec), check_vma=False)
```

profile of v0, /device:TPU:1, one launch (start us, length us, event | category | flops | bytes accessed | tf_op | source)
XLA Modules:
  0.0 92.5 jit_solution(5485027095271233806)
XLA Ops:
  0.6 89.2 %attend.1.packed_ref = bf16[4,8,128,128]{3,2,1,0:T(8,128)(2,1)} custom-call(bf16[128,1024]{1,0:T(8,128)(2,1)} %q_ref.1, bf16[128,1024]{1,0:T(8,128)(2,1)} %k_ref.1, bf16[128,1024]{1,0:T(8,128)(2,1)} %v_ref.1, bf16[128,1024]{1,0:T(8,128)(2,1)} %do_ref.1, s32[256,128]{1,0:T(8,128)} %bitcast.1), custom_call_target="tpu_custom_call" | custom-call | tf_op jit(solution)/shard_map/attend/pallas_call | solution.py:452
  89.8 0.0 copy-start
  89.8 1.2 %copy-done = bf16[4,8,128,128]{3,2,1,0:T(8,128)(2,1)S(1)} copy-done((bf16[4,8,128,128]{3,2,1,0:T(8,128)(2,1)S(1)}, bf16[4,8,128,128]{3,2,1,0:T(8,128)(2,1)}, u32[]{:S(2)}) %copy-start) | copy-done | bytes 1048600
  91.0 1.5 %restore.1 = (bf16[128,1024]{1,0:T(8,128)(2,1)}, bf16[128,1024]{1,0:T(8,128)(2,1)}, bf16[128,1024]{1,0:T(8,128)(2,1)}, bf16[128,1024]{1,0:T(8,128)(2,1)}) custom-call(bf16[4,8,128,128]{3,2,1,0:T(8,128)(2,1)S(1)} %copy-done), custom_call_target="tpu_custom_call" | custom-call | tf_op jit(solution)/shard_map/restore/pallas_call | solution.py:495
Async XLA Ops:
  89.8 1.2 %copy-start = (bf16[4,8,128,128]{3,2,1,0:T(8,128)(2,1)S(1)}, bf16[4,8,128,128]{3,2,1,0:T(8,128)(2,1)}, u32[]{:S(2)}) copy-start(bf16[4,8,128,128]{3,2,1,0:T(8,128)(2,1)} %attend.1.packed_ref) | copy-start | bytes 3145732
where the time goes:
time: 92.7 us; the launch traced here: 92.5 us
  Pallas kernels  90.7 us (98%)
  local copies, waits for them, and re-layouts  1.22 us (1%)
    pallas_call x1, Pallas kernels, body(): pl.pallas_call(attend_kernel, out_shape=jax.ShapeDtypeStruct((4, NH, NB,...  89.2 us

commit v1 on v0

v1 whole, which is shorter than its diff:
```python
import jax
import jax.numpy as jnp
from jax import lax
from jax.experimental import pallas as pl
from jax.experimental.pallas import tpu as pltpu
from jax.sharding import PartitionSpec as P

F32 = jnp.float32
BF16 = jnp.bfloat16
I32 = jnp.int32
BIG = 1e30
NH = 8
NB = 128
MESH = pl.DeviceIdType.MESH
ROW_O, ROW_Q, ROW_KV, ROW_T8, ROW_TZ, ROWS = (0, 64), (128, 192), (256, 384), (512, 528), (544, 560), 576


def iota(shape, dim):
    return lax.broadcasted_iota(I32, shape, dim)


def token_of(parity, w, h):
    t, u, a = (w >> 4) & 3, (w >> 2) & 3, w & 3
    return a * 32 + parity + 2 * ((h + t) & 3) + 8 * ((h // 4 + u) & 3)


def nn(a, b):
    return lax.dot_general(a, b, (((1,), (0,)), ((), ())), preferred_element_type=F32)


def attend_kernel(
    q_hbm, k_hbm, v_hbm, do_hbm, docs_hbm, out_ref,
    q_ref, k_ref, v_ref, do_ref, docs_ref,
    send, inbuf, zin, kv2, kv8, kv32, KX, KVT, QG, QXT, QXT32, QM, DOM, DOT,
    ST, OT, DQT, ACC, g2, r2, g8, r8, g32, r32, og,
    load_s, in_ss, in_rs, zin_ss, zin_rs, loc_s, l2_ss, l2_rs, l8_ss, l8_rs, l32_ss, l32_rs,
    out_ss, out_rs, tz_ss, tz_rs, out_loc,
):
    h = lax.axis_index("head")
    s = lax.axis_index("seq")
    pair = s + 1 - 2 * (s % 2)
    base8 = (s // 8) * 8
    base16 = (s // 16) * 16
    zpeer = (s + 16) % 32

    def plane_peer(k):
        return base16 + (s - base16 + k) % 16

    def oct_peer(k):
        return base8 + (s - base8 + k) % 8

    def head_peer(k):
        return (h + k) % NH

    barrier = pltpu.get_barrier_semaphore()
    for k in range(1, NH):
        pl.semaphore_signal(barrier, inc=1, device_id={"head": head_peer(k)}, device_id_type=MESH)
    for k in range(1, 16):
        pl.semaphore_signal(barrier, inc=1, device_id={"seq": plane_peer(k)}, device_id_type=MESH)
    for k in range(NH):
        pl.semaphore_signal(barrier, inc=1, device_id={"seq": zpeer, "head": head_peer(k)}, device_id_type=MESH)

    pairs = ((k_hbm, k_ref), (v_hbm, v_ref), (q_hbm, q_ref), (do_hbm, do_ref), (docs_hbm, docs_ref))
    loads = [pltpu.make_async_copy(a, b, load_s.at[i]) for i, (a, b) in enumerate(pairs)]
    for load in loads:
        load.start()

    lane128 = iota((128, 128), 1)
    row128 = iota((128, 128), 0)
    low = lane128 < 64

    def permute_two(first, a_ref, b_ref):
        for g in range(NH):
            mat = (lane128 == token_of(row128 >> 6, row128 & 63, g)).astype(F32).astype(BF16)
            cols = slice(g * 128, g * 128 + 128)
            res = nn(mat, jnp.concatenate([a_ref[:, cols], b_ref[:, cols]], axis=1))
            a, b = res[:, 0:128], res[:, 128:256]
            send[first, g] = jnp.where(low, a, pltpu.roll(b, 64, 1)).astype(BF16)
            other = jnp.where(low, pltpu.roll(a, 64, 1), b).astype(BF16)
            send[first + 2, g, 0:64] = other[64:128]
            send[first + 2, g, 64:128] = other[0:64]

    def in_copy(t, k):
        return pltpu.make_async_remote_copy(
            src_ref=send.at[t, head_peer(k)], dst_ref=inbuf.at[t, h],
            send_sem=in_ss.at[t * 7 + k - 1], recv_sem=in_rs.at[t * 7 + k - 1],
            device_id={"head": head_peer(k)}, device_id_type=MESH)

    def in_local(t):
        return pltpu.make_async_copy(send.at[t, h], inbuf.at[t, h], loc_s.at[t])

    def start_in(t):
        for k in range(1, NH):
            in_copy(t, k).start()
        in_local(t).start()

    def wait_in(t):
        for k in range(1, NH):
            in_copy(t, k).wait_recv()
        in_local(t).wait()

    def zin_copy(j, k):
        return pltpu.make_async_remote_copy(
            src_ref=send.at[2 * j, head_peer(k), pl.ds(0, 16)], dst_ref=zin.at[j, h],
            send_sem=zin_ss.at[8 * j + k], recv_sem=zin_rs.at[8 * j + k],
            device_id={"seq": zpeer, "head": head_peer(k)}, device_id_type=MESH)

    def start_keys(j):
        for k in range(NH):
            zin_copy(j, k).start()
        start_in(2 * j)

    loads[0].wait()
    loads[1].wait()
    permute_two(0, k_ref, v_ref)
    loads[2].wait()
    loads[3].wait()
    permute_two(1, q_ref, do_ref)
    pl.semaphore_wait(barrier, 30)
    start_keys(0)
    start_in(1)
    loads[4].wait()

    docs = docs_ref[...]

    def count(limit):
        c = jnp.sum((docs < limit).astype(F32), axis=0, keepdims=True)
        return jnp.sum(c, axis=1, keepdims=True).astype(I32)

    bound1, bound2 = count(1), count(2)

    def doc_of(pos):
        return (pos >= bound1).astype(I32) + (pos >= bound2).astype(I32)

    def key_place(level, c):
        r = row128 + c * 128
        if level == 0:
            return s, r >> 7, r & 127
        if level == 1:
            return jnp.where((r >> 9) == 0, s, pair), (r >> 6) & 7, r & 63
        if level == 2:
            return base8 + ((s + (r >> 7)) & 7), (r >> 4) & 7, r & 15
        plane = jnp.where(((r >> 5) & 1) == 0, base16, 16 - base16)
        return plane + ((s + (r >> 6)) & 15), (r >> 2) & 7, r & 3

    def fill_features(c, carry):
        for level in range(4):
            seqs, src, w = key_place(level, c)
            start = seqs * 1024 + src * 128
            for j in range(2):
                parity = j ^ (w >> 6)
                doc = doc_of(start + token_of(parity, w & 63, h))
                hot = (lane128 - 64 == doc) | (lane128 == 67)
                KX[level, j, pl.ds(c * 128, 128)] = jnp.where(hot, 1.0, 0.0).astype(BF16)
        return carry

    lax.fori_loop(0, 8, fill_features, 0)

    feat_row = row128 - 64
    for c in range(8):
        if c % 4 == 0:
            src, w = lane128 >> 4, lane128 & 15
        else:
            i = lane128 + (c % 4 - 1) * 128
            src = (i * 1366) >> 16
            w = 16 + i - src * 48
        w = w + 64 * (c // 4)
        for j in range(2):
            parity = j ^ (w >> 6)
            doc = doc_of(s * 1024 + src * 128 + token_of(parity, w & 63, h))
            hide = (feat_row >= 0) & (feat_row < 3) & (feat_row != doc)
            QXT[j, c] = jnp.where(hide, -BIG, 0.0).astype(BF16)
            if c == 0:
                hide = hide | ((feat_row == 3) & (w >= 4))
                QXT32[j] = jnp.where(hide, -BIG, 0.0).astype(BF16)

    ACC[...] = jnp.zeros(ACC.shape, F32)
    DQT[...] = jnp.zeros(DQT.shape, F32)

    def l2_copy(j):
        return pltpu.make_async_remote_copy(
            src_ref=inbuf.at[2 * j, :, pl.ds(0, 64), :], dst_ref=kv2.at[j, 1],
            send_sem=l2_ss.at[j], recv_sem=l2_rs.at[j], device_id={"seq": pair}, device_id_type=MESH)

    def l8_copy(j, k):
        return pltpu.make_async_remote_copy(
            src_ref=inbuf.at[2 * j, :, pl.ds(0, 16), :], dst_ref=kv8.at[j, 8 - k],
            send_sem=l8_ss.at[7 * j + k - 1], recv_sem=l8_rs.at[7 * j + k - 1],
            device_id={"seq": oct_peer(k)}, device_id_type=MESH)

    def l32_copy(j, k):
        return pltpu.make_async_remote_copy(
            src_ref=kv32.at[j, 0], dst_ref=kv32.at[j, 16 - k],
            send_sem=l32_ss.at[15 * j + k - 1], recv_sem=l32_rs.at[15 * j + k - 1],
            device_id={"seq": plane_peer(k)}, device_id_type=MESH)

    pick_row, pick_col = iota((32, 128), 0), iota((32, 128), 1)
    pick = (pick_col == (pick_row >> 2) * 16 + (pick_row & 3)).astype(F32).astype(BF16)

    def start_levels(j):
        l2_copy(j).start()
        for k in range(1, 8):
            l8_copy(j, k).start()
        for k in range(NH):
            zin_copy(j, k).wait_recv()
        kv32[j, 0, 0] = nn(pick, inbuf[2 * j, :, 0:16].reshape(128, 128)).astype(BF16)
        kv32[j, 0, 1] = nn(pick, zin[j].reshape(128, 128)).astype(BF16)
        for k in range(1, 16):
            l32_copy(j, k).start()
        kv2[j, 0] = inbuf[2 * j, :, 0:64]
        kv8[j, 0] = inbuf[2 * j, :, 0:16]

    def prepare(level, j, load):
        def chunk(c, carry):
            rows = pl.ds(pl.multiple_of(c * 128, 128), 128)
            kv = load(c).astype(F32)
            KX[level, j, rows] = jnp.where(low, kv, KX[level, j, rows].astype(F32)).astype(BF16)
            KVT[level, j, :, rows] = kv.T.astype(BF16)
            return carry

        lax.fori_loop(0, 8, chunk, 0)

    def natural(level, j):
        ref = (inbuf.at[2 * j], kv2.at[j], kv8.at[j], kv32.at[j])[level]
        return ref[...].reshape(1024, 128)

    def prepare_queries(j):
        x = inbuf.at[2 * j + 1]
        QG[0:128] = x[:, 0:16].reshape(128, 128)
        QG[128:512] = x[:, 16:64].reshape(384, 128)
        QG[512:640] = x[:, 64:80].reshape(128, 128)
        QG[640:1024] = x[:, 80:128].reshape(384, 128)
        for c in range(8):
            rows = slice(c * 128, c * 128 + 128)
            qd = QG[rows].astype(F32)
            query, up = qd * 0.125, jnp.where(low, 0.0, qd)
            query_t = query.T
            QM[j, rows] = jnp.where(low, query, 0.0).astype(BF16)
            DOM[j, rows] = up.astype(BF16)
            DOT[j, c] = up.T.astype(BF16)
            QXT[j, c] = jnp.where(row128 < 64, query_t, QXT[j, c].astype(F32)).astype(BF16)
            if c == 0:
                QXT32[j] = jnp.where(row128 < 64, query_t, QXT32[j].astype(F32)).astype(BF16)

    def wide(ref, j, b):
        return jnp.concatenate([ref[j, 4 * b + i] for i in range(4)], axis=1)

    def forward(level, j, qxt):
        sc = nn(KX[level, j], qxt)
        m = jnp.max(sc, axis=0, keepdims=True)
        w = jnp.exp(sc - m)
        total = jnp.sum(w, axis=0, keepdims=True)
        o = nn(KVT[level, j, 64:128], w.astype(BF16))
        return m, total, o

    def merge(j, b, width, m, total, o):
        m0, l0, o0 = ST[0, j, b, :, :width], ST[1, j, b, :, :width], OT[j, b, :, :width]
        mm = jnp.maximum(m0, m)
        e0, e1 = jnp.exp(m0 - mm), jnp.exp(m - mm)
        ST[0, j, b, :, :width] = mm
        ST[1, j, b, :, :width] = l0 * e0 + total * e1
        OT[j, b, :, :width] = o0 * e0 + o * e1

    def forward_first(j):
        def step(i, carry):
            m, total, o = forward(0, j, wide(QXT, j, i))
            ST[0, j, i] = m
            ST[1, j, i] = total
            OT[j, i] = o
            return carry

        lax.fori_loop(0, 2, step, 0)

    def forward_rest(j):
        l2_copy(j).wait()
        prepare(1, j, lambda c: kv2[j, c // 4, pl.ds((c % 4) * 2, 2)].reshape(128, 128))
        merge(j, 0, 512, *forward(1, j, wide(QXT, j, 0)))
        for k in range(1, 8):
            l8_copy(j, k).wait()
        prepare(2, j, lambda c: kv8[j, c].reshape(128, 128))
        merge(j, 0, 128, *forward(2, j, QXT[j, 0]))
        for k in range(1, 16):
            l32_copy(j, k).wait()
        prepare(3, j, lambda c: kv32[j, pl.ds(2 * c, 2)].reshape(128, 128))
        merge(j, 0, 128, *forward(3, j, QXT32[j]))
        for b in range(2):
            total = ST[1, j, b]
            o = OT[j, b] / total
            OT[j, b] = o
            ST[0, j, b] = ST[0, j, b] + jnp.log(total)
            ST[1, j, b] = jnp.sum(wide(DOT, j, b)[64:128].astype(F32) * o, axis=0, keepdims=True)

    def out_copy(i, src, row, n, k):
        return pltpu.make_async_remote_copy(
            src_ref=src.at[head_peer(k)], dst_ref=out_ref.at[h, pl.ds(row, n)],
            send_sem=out_ss.at[i * 7 + k - 1], recv_sem=out_rs.at[i * 7 + k - 1],
            device_id={"head": head_peer(k)}, device_id_type=MESH)

    def out_local(i, src, row, n):
        return pltpu.make_async_copy(src.at[h], out_ref.at[h, pl.ds(row, n)], out_loc.at[i])

    def og_part(row, n):
        return og.at[:, pl.ds(row, n)]

    parts = []
    for j in range(2):
        parts += [(ROW_O[j], 64), (ROW_Q[j], 64), (ROW_KV[j], 128), (ROW_T8[j], 16)]

    def start_out(i):
        row, n = parts[i]
        for k in range(1, NH):
            out_copy(i, og_part(row, n), row, n, k).start()
        out_local(i, og_part(row, n), row, n).start()

    def tz_copy(j, k):
        return pltpu.make_async_remote_copy(
            src_ref=og.at[head_peer(k), pl.ds(ROW_TZ[j], 16)], dst_ref=out_ref.at[h, pl.ds(ROW_TZ[j], 16)],
            send_sem=tz_ss.at[8 * j + k], recv_sem=tz_rs.at[8 * j + k],
            device_id={"seq": zpeer, "head": head_peer(k)}, device_id_type=MESH)

    def send_rows(i, top, bottom):
        row = parts[i][0]
        both = jnp.concatenate([top, bottom], axis=0).T.astype(BF16)
        og[:, row:row + 16] = both[0:128].reshape(8, 16, 128)
        og[:, row + 16:row + 64] = both[128:512].reshape(8, 48, 128)
        start_out(i)

    def backward(level, j, b, width, qxt, dot_t, rows):
        p = jnp.exp(nn(KX[level, j], qxt) - ST[0, j, b, :, :width])
        dp = nn(natural(level, j), dot_t)
        ds = (p * (dp - ST[1, j, b, :, :width])).astype(BF16)
        ACC[level, j] += nn(ds, QM[j, rows]) + nn(p.astype(BF16), DOM[j, rows])
        DQT[j, b, :, :width] += nn(KVT[level, j, 0:64], ds)

    def g32_copy(j, k):
        return pltpu.make_async_remote_copy(
            src_ref=g32.at[j, k], dst_ref=r32.at[j, 16 - k],
            send_sem=l32_ss.at[29 + 15 * j + k], recv_sem=l32_rs.at[29 + 15 * j + k],
            device_id={"seq": plane_peer(k)}, device_id_type=MESH)

    def g8_copy(j, k):
        return pltpu.make_async_remote_copy(
            src_ref=g8.at[j, k], dst_ref=r8.at[j, 8 - k],
            send_sem=l8_ss.at[13 + 7 * j + k], recv_sem=l8_rs.at[13 + 7 * j + k],
            device_id={"seq": oct_peer(k)}, device_id_type=MESH)

    def g2_copy(j):
        return pltpu.make_async_remote_copy(
            src_ref=g2.at[j], dst_ref=r2.at[j], send_sem=l2_ss.at[2 + j], recv_sem=l2_rs.at[2 + j],
            device_id={"seq": pair}, device_id_type=MESH)

    def backward_sparse(j):
        backward(3, j, 0, 128, QXT32[j], DOT[j, 0], pl.ds(0, 128))
        g32[j] = ACC[3, j].reshape(16, 2, 32, 128).astype(BF16)
        for k in range(1, 16):
            g32_copy(j, k).start()
        backward(2, j, 0, 128, QXT[j, 0], DOT[j, 0], pl.ds(0, 128))
        g8[j] = ACC[2, j].reshape(8, 128, 128).astype(BF16)
        for k in range(1, 8):
            g8_copy(j, k).start()

    def backward_pair(j):
        backward(1, j, 0, 512, wide(QXT, j, 0), wide(DOT, j, 0), pl.ds(0, 512))
        g2[j] = ACC[1, j, 512:1024].reshape(8, 64, 128).astype(BF16)
        g2_copy(j).start()

    def backward_local(j):
        def step(i, carry):
            rows = pl.ds(pl.multiple_of(i * 512, 512), 512)
            backward(0, j, i, 512, wide(QXT, j, i), wide(DOT, j, i), rows)
            return carry

        lax.fori_loop(0, 2, step, 0)

    put_row, put_col = iota((128, 32), 0), iota((128, 32), 1)
    put = (put_row == (put_col >> 2) * 16 + (put_col & 3)).astype(F32).astype(BF16)

    def send_keys(j):
        g2_copy(j).wait()
        for b in range(8):
            t2 = ACC[1, j, b * 64:b * 64 + 64] + r2[j, b].astype(F32)
            own = ACC[0, j, b * 128:b * 128 + 128]
            og[b, ROW_KV[j]:ROW_KV[j] + 64] = (own[0:64] + t2).astype(BF16)
            og[b, ROW_KV[j] + 64:ROW_KV[j] + 128] = own[64:128].astype(BF16)
        start_out(4 * j + 2)

    def spread(x):
        hi = x.astype(BF16)
        return nn(put, hi) + nn(put, (x - hi.astype(F32)).astype(BF16))

    def send_tiles(j):
        for k in range(1, 16):
            g32_copy(j, k).wait()
        mine, theirs = ACC[3, j, 0:32], ACC[3, j, 32:64]
        for m in range(1, 16):
            mine += r32[j, m, 0].astype(F32)
            theirs += r32[j, m, 1].astype(F32)
        og[:, ROW_TZ[j]:ROW_TZ[j] + 16] = spread(theirs).astype(BF16).reshape(8, 16, 128)
        for k in range(NH):
            tz_copy(j, k).start()
        for k in range(1, 8):
            g8_copy(j, k).wait()
        t8 = ACC[2, j, 0:128] + spread(mine)
        for m in range(1, 8):
            t8 += r8[j, m].astype(F32)
        og[:, ROW_T8[j]:ROW_T8[j] + 16] = t8.astype(BF16).reshape(8, 16, 128)
        start_out(4 * j + 3)

    def prepare_local(j):
        prepare(0, j, lambda c: inbuf[2 * j, c])

    def send_output(j):
        send_rows(4 * j, OT[j, 0], OT[j, 1])

    def send_queries(j):
        send_rows(4 * j + 1, DQT[j, 0] * 0.125, DQT[j, 1] * 0.125)

    wait_in(0)
    start_keys(1)
    start_levels(0)
    prepare_local(0)
    wait_in(1)
    start_in(3)
    prepare_queries(0)
    forward_first(0)
    forward_rest(0)
    send_output(0)
    wait_in(2)
    start_levels(1)
    backward_pair(0)
    backward_sparse(0)
    prepare_local(1)
    backward_local(0)
    send_queries(0)
    wait_in(3)
    prepare_queries(1)
    forward_first(1)
    send_keys(0)
    send_tiles(0)
    forward_rest(1)
    send_output(1)
    backward_pair(1)
    backward_sparse(1)
    backward_local(1)
    send_queries(1)
    send_keys(1)
    send_tiles(1)

    for t in range(4):
        for k in range(1, NH):
            in_copy(t, k).wait_send()
    for j in range(2):
        for k in range(NH):
            zin_copy(j, k).wait_send()
            tz_copy(j, k).wait()
    for i, (row, n) in enumerate(parts):
        for k in range(1, NH):
            out_copy(i, og_part(row, n), row, n, k).wait()
        out_local(i, og_part(row, n), row, n).wait()


def restore_kernel(packed_ref, a_ref, q_ref, k_ref, v_ref):
    low = iota((128, 128), 1) < 64
    low64 = iota((64, 128), 1) < 64
    for g in range(NH):
        rho = iota((NB, NB), 1)
        mat = (iota((NB, NB), 0) == token_of(rho >> 6, rho & 63, g)).astype(F32).astype(BF16)
        cols = []
        for rows in (ROW_O, ROW_Q):
            x, y = (packed_ref[g, row:row + 64].astype(F32) for row in rows)
            odd = pltpu.roll(jnp.where(low64, y, x), 64, 1)
            cols.append(jnp.concatenate([jnp.where(low64, x, y), odd], axis=0).astype(BF16))
        for j in range(2):
            tile = sum(packed_ref[g, row:row + 16].astype(F32) for row in (ROW_KV[j], ROW_T8[j], ROW_TZ[j]))
            own = [tile.astype(BF16), packed_ref[g, ROW_KV[j] + 16:ROW_KV[j] + 64]]
            other = [packed_ref[g, ROW_KV[j] + 64:ROW_KV[j] + 128]]
            cols.append(jnp.concatenate(other + own if j else own + other, axis=0))
        res = nn(mat, jnp.concatenate(cols, axis=1))
        here = slice(g * 128, g * 128 + 128)
        a_ref[:, here] = res[:, 0:128].astype(BF16)
        q_ref[:, here] = res[:, 128:256].astype(BF16)
        x, y = res[:, 256:384], res[:, 384:512]
        k_ref[:, here] = jnp.where(low, x, pltpu.roll(y, 64, 1)).astype(BF16)
        v_ref[:, here] = jnp.where(low, pltpu.roll(x, 64, 1), y).astype(BF16)


def body(queries, keys, values, grad_out, doc_ids):
    vmem = pl.BlockSpec(memory_space=pltpu.VMEM)
    dma = pltpu.SemaphoreType.DMA
    packed = pl.pallas_call(
        attend_kernel,
        out_shape=jax.ShapeDtypeStruct((NH, ROWS, 128), BF16),
        in_specs=[pl.BlockSpec(memory_space=pl.ANY)] * 5,
        out_specs=pl.BlockSpec(memory_space=pl.ANY),
        scratch_shapes=[pltpu.VMEM(queries.shape, BF16)] * 4 + [
            pltpu.VMEM((256, 128), I32),
            pltpu.VMEM((4, NH, NB, 128), BF16),
            pltpu.VMEM((4, NH, NB, 128), BF16),
            pltpu.VMEM((2, 8, 16, 128), BF16),
            pltpu.VMEM((2, 2, 8, 64, 128), BF16),
            pltpu.VMEM((2, 8, 8, 16, 128), BF16),
            pltpu.VMEM((2, 16, 2, 32, 128), BF16),
            pltpu.VMEM((4, 2, 1024, 128), BF16),
            pltpu.VMEM((4, 2, 128, 1024), BF16),
            pltpu.VMEM((1024, 128), BF16),
            pltpu.VMEM((2, 8, 128, 128), BF16),
            pltpu.VMEM((2, 128, 128), BF16),
            pltpu.VMEM((2, 1024, 128), BF16),
            pltpu.VMEM((2, 1024, 128), BF16),
            pltpu.VMEM((2, 8, 128, 128), BF16),
            pltpu.VMEM((2, 2, 2, 1, 512), F32),
            pltpu.VMEM((2, 2, 64, 512), F32),
            pltpu.VMEM((2, 2, 64, 512), F32),
            pltpu.VMEM((4, 2, 1024, 128), F32),
            pltpu.VMEM((2, 8, 64, 128), BF16),
            pltpu.VMEM((2, 8, 64, 128), BF16),
            pltpu.VMEM((2, 8, 128, 128), BF16),
            pltpu.VMEM((2, 8, 128, 128), BF16),
            pltpu.VMEM((2, 16, 2, 32, 128), BF16),
            pltpu.VMEM((2, 16, 2, 32, 128), BF16),
            pltpu.VMEM((NH, ROWS, 128), BF16),
            dma((5,)), dma((28,)), dma((28,)), dma((16,)), dma((16,)), dma((4,)),
            dma((4,)), dma((4,)), dma((28,)), dma((28,)), dma((60,)), dma((60,)),
            dma((56,)), dma((56,)), dma((16,)), dma((16,)), dma((8,)),
        ],
        compiler_params=pltpu.CompilerParams(
            collective_id=0, has_side_effects=True, vmem_limit_bytes=56 * 1024 * 1024),
        name="attend",
    )(queries, keys, values, grad_out, doc_ids.reshape(256, 128))
    shape = jax.ShapeDtypeStruct(queries.shape, BF16)
    return pl.pallas_call(
        restore_kernel,
        out_shape=(shape, shape, shape, shape),
        in_specs=[vmem],
        out_specs=(vmem, vmem, vmem, vmem),
        compiler_params=pltpu.CompilerParams(vmem_limit_bytes=32 * 1024 * 1024),
        name="restore",
    )(packed)


def solution(mesh):
    spec = P(("seq", "head"), None)
    return jax.shard_map(
        body, mesh=mesh, in_specs=(spec, spec, spec, spec, P()), out_specs=(spec, spec, spec, spec), check_vma=False)
```

time: 92.7 us -> 86 us (0.928)
  Pallas kernels: 90.7 us -> 84 us
    pallas_call x1, Pallas kernels: 89.2 us -> 82.5 us  [body(): pl.pallas_call(attend_kernel, out_shape=jax.ShapeDtypeStruct((NH, ROWS, 1...]
where the time goes in v1:
time: 86 us; the launch traced here: 85.9 us
  Pallas kernels  84 us (98%)
  local copies, waits for them, and re-layouts  1.26 us (1%)
    pallas_call x1, Pallas kernels, body(): pl.pallas_call(attend_kernel, out_shape=jax.ShapeDtypeStruct((NH, ROWS, 1...  82.5 us

profile of v1, /device:TPU:1, one launch (start us, length us, event | category | flops | bytes accessed | tf_op | source)
XLA Modules:
  0.0 85.9 jit_solution(13670879863440323272)
XLA Ops:
  0.6 82.5 %attend.1.packed_ref = bf16[8,576,128]{2,1,0:T(8,128)(2,1)} custom-call(bf16[128,1024]{1,0:T(8,128)(2,1)} %q_hbm.1, bf16[128,1024]{1,0:T(8,128)(2,1)} %k_hbm.1, bf16[128,1024]{1,0:T(8,128)(2,1)} %v_hbm.1, bf16[128,1024]{1,0:T(8,128)(2,1)} %do_hbm.1, s32[256,128]{1,0:T(8,128)} %bitcast.1), custom_call_target="tpu_custom_call" | custom-call | tf_op jit(solution)/shard_map/attend/pallas_call | solution.py:490
  83.1 0.0 copy-start
  83.1 1.3 %copy-done = bf16[8,576,128]{2,1,0:T(8,128)(2,1)S(1)} copy-done((bf16[8,576,128]{2,1,0:T(8,128)(2,1)S(1)}, bf16[8,576,128]{2,1,0:T(8,128)(2,1)}, u32[]{:S(2)}) %copy-start) | copy-done | bytes 1179672
  84.4 1.5 %restore.1 = (bf16[128,1024]{1,0:T(8,128)(2,1)}, bf16[128,1024]{1,0:T(8,128)(2,1)}, bf16[128,1024]{1,0:T(8,128)(2,1)}, bf16[128,1024]{1,0:T(8,128)(2,1)}) custom-call(bf16[8,576,128]{2,1,0:T(8,128)(2,1)S(1)} %copy-done), custom_call_target="tpu_custom_call" | custom-call | tf_op jit(solution)/shard_map/restore/pallas_call | solution.py:531
Async XLA Ops:
  83.1 1.3 %copy-start = (bf16[8,576,128]{2,1,0:T(8,128)(2,1)S(1)}, bf16[8,576,128]{2,1,0:T(8,128)(2,1)}, u32[]{:S(2)}) copy-start(bf16[8,576,128]{2,1,0:T(8,128)(2,1)} %attend.1.packed_ref) | copy-start | bytes 3538948

commit v2 on v1

--- a/solution.py
+++ b/solution.py
@@ -12,7 +12,7 @@
 NH = 8
 NB = 128
 MESH = pl.DeviceIdType.MESH
-ROW_O, ROW_Q, ROW_KV, ROW_T8, ROW_TZ, ROWS = (0, 64), (128, 192), (256, 384), (512, 528), (544, 560), 576
+ROW_Q, ROW_KV, ROW_T8, ROW_TZ, ROWS = ((0, 64), (128, 192)), (256, 384), (512, 528), (544, 560), 576
 
 
 def iota(shape, dim):
@@ -32,7 +32,7 @@
     q_hbm, k_hbm, v_hbm, do_hbm, docs_hbm, out_ref,
     q_ref, k_ref, v_ref, do_ref, docs_ref,
     send, inbuf, zin, kv2, kv8, kv32, KX, KVT, QG, QXT, QXT32, QM, DOM, DOT,
-    ST, OT, DQT, ACC, g2, r2, g8, r8, g32, r32, og,
+    W1, W2, W8, W32, ACC, g2, r2, g8, r8, g32, r32, og,
     load_s, in_ss, in_rs, zin_ss, zin_rs, loc_s, l2_ss, l2_rs, l8_ss, l8_rs, l32_ss, l32_rs,
     out_ss, out_rs, tz_ss, tz_rs, out_loc,
 ):
@@ -80,24 +80,29 @@
             send[first + 2, g, 0:64] = other[64:128]
             send[first + 2, g, 64:128] = other[0:64]
 
-    def in_copy(t, k):
-        return pltpu.make_async_remote_copy(
-            src_ref=send.at[t, head_peer(k)], dst_ref=inbuf.at[t, h],
-            send_sem=in_ss.at[t * 7 + k - 1], recv_sem=in_rs.at[t * 7 + k - 1],
+    messages = ((0, 0, 128), (1, 64, 64), (2, 0, 128), (1, 0, 64), (3, 0, 64), (3, 64, 64))
+
+    def in_copy(i, k):
+        t, row, n = messages[i]
+        return pltpu.make_async_remote_copy(
+            src_ref=send.at[t, head_peer(k), pl.ds(row, n)], dst_ref=inbuf.at[t, h, pl.ds(row, n)],
+            send_sem=in_ss.at[i * 7 + k - 1], recv_sem=in_rs.at[i * 7 + k - 1],
             device_id={"head": head_peer(k)}, device_id_type=MESH)
 
-    def in_local(t):
-        return pltpu.make_async_copy(send.at[t, h], inbuf.at[t, h], loc_s.at[t])
-
-    def start_in(t):
+    def in_local(i):
+        t, row, n = messages[i]
+        return pltpu.make_async_copy(
+            send.at[t, h, pl.ds(row, n)], inbuf.at[t, h, pl.ds(row, n)], loc_s.at[i])
+
+    def start_in(i):
         for k in range(1, NH):
-            in_copy(t, k).start()
-        in_local(t).start()
-
-    def wait_in(t):
+            in_copy(i, k).start()
+        in_local(i).start()
+
+    def wait_in(i):
         for k in range(1, NH):
-            in_copy(t, k).wait_recv()
-        in_local(t).wait()
+            in_copy(i, k).wait_recv()
+        in_local(i).wait()
 
     def zin_copy(j, k):
         return pltpu.make_async_remote_copy(
@@ -105,20 +110,23 @@
             send_sem=zin_ss.at[8 * j + k], recv_sem=zin_rs.at[8 * j + k],
             device_id={"seq": zpeer, "head": head_peer(k)}, device_id_type=MESH)
 
-    def start_keys(j):
+    def start_zin(j):
         for k in range(NH):
             zin_copy(j, k).start()
-        start_in(2 * j)
 
     loads[0].wait()
     loads[1].wait()
     permute_two(0, k_ref, v_ref)
+    pl.semaphore_wait(barrier, 30)
+    start_zin(0)
+    start_in(0)
     loads[2].wait()
     loads[3].wait()
     permute_two(1, q_ref, do_ref)
-    pl.semaphore_wait(barrier, 30)
-    start_keys(0)
     start_in(1)
+    start_zin(1)
+    for i in range(2, 6):
+        start_in(i)
     loads[4].wait()
 
     docs = docs_ref[...]
@@ -174,9 +182,6 @@
                 hide = hide | ((feat_row == 3) & (w >= 4))
                 QXT32[j] = jnp.where(hide, -BIG, 0.0).astype(BF16)
 
-    ACC[...] = jnp.zeros(ACC.shape, F32)
-    DQT[...] = jnp.zeros(DQT.shape, F32)
-
     def l2_copy(j):
         return pltpu.make_async_remote_copy(
             src_ref=inbuf.at[2 * j, :, pl.ds(0, 64), :], dst_ref=kv2.at[j, 1],
@@ -224,15 +229,14 @@
         ref = (inbuf.at[2 * j], kv2.at[j], kv8.at[j], kv32.at[j])[level]
         return ref[...].reshape(1024, 128)
 
-    def prepare_queries(j):
-        x = inbuf.at[2 * j + 1]
+    def prepare_queries(j, part):
+        x = inbuf.at[2 * j + 1, :, pl.ds(64 * part, 64)]
         QG[0:128] = x[:, 0:16].reshape(128, 128)
         QG[128:512] = x[:, 16:64].reshape(384, 128)
-        QG[512:640] = x[:, 64:80].reshape(128, 128)
-        QG[640:1024] = x[:, 80:128].reshape(384, 128)
-        for c in range(8):
+        for i in range(4):
+            c = 4 * part + i
             rows = slice(c * 128, c * 128 + 128)
-            qd = QG[rows].astype(F32)
+            qd = QG[i * 128:i * 128 + 128].astype(F32)
             query, up = qd * 0.125, jnp.where(low, 0.0, qd)
             query_t = query.T
             QM[j, rows] = jnp.where(low, query, 0.0).astype(BF16)
@@ -245,50 +249,20 @@
     def wide(ref, j, b):
         return jnp.concatenate([ref[j, 4 * b + i] for i in range(4)], axis=1)
 
-    def forward(level, j, qxt):
+    def forward(level, j, qxt, weights):
         sc = nn(KX[level, j], qxt)
         m = jnp.max(sc, axis=0, keepdims=True)
         w = jnp.exp(sc - m)
+        weights[...] = w
         total = jnp.sum(w, axis=0, keepdims=True)
         o = nn(KVT[level, j, 64:128], w.astype(BF16))
         return m, total, o
 
-    def merge(j, b, width, m, total, o):
-        m0, l0, o0 = ST[0, j, b, :, :width], ST[1, j, b, :, :width], OT[j, b, :, :width]
-        mm = jnp.maximum(m0, m)
-        e0, e1 = jnp.exp(m0 - mm), jnp.exp(m - mm)
-        ST[0, j, b, :, :width] = mm
-        ST[1, j, b, :, :width] = l0 * e0 + total * e1
-        OT[j, b, :, :width] = o0 * e0 + o * e1
-
-    def forward_first(j):
-        def step(i, carry):
-            m, total, o = forward(0, j, wide(QXT, j, i))
-            ST[0, j, i] = m
-            ST[1, j, i] = total
-            OT[j, i] = o
-            return carry
-
-        lax.fori_loop(0, 2, step, 0)
-
-    def forward_rest(j):
-        l2_copy(j).wait()
-        prepare(1, j, lambda c: kv2[j, c // 4, pl.ds((c % 4) * 2, 2)].reshape(128, 128))
-        merge(j, 0, 512, *forward(1, j, wide(QXT, j, 0)))
-        for k in range(1, 8):
-            l8_copy(j, k).wait()
-        prepare(2, j, lambda c: kv8[j, c].reshape(128, 128))
-        merge(j, 0, 128, *forward(2, j, QXT[j, 0]))
-        for k in range(1, 16):
-            l32_copy(j, k).wait()
-        prepare(3, j, lambda c: kv32[j, pl.ds(2 * c, 2)].reshape(128, 128))
-        merge(j, 0, 128, *forward(3, j, QXT32[j]))
-        for b in range(2):
-            total = ST[1, j, b]
-            o = OT[j, b] / total
-            OT[j, b] = o
-            ST[0, j, b] = ST[0, j, b] + jnp.log(total)
-            ST[1, j, b] = jnp.sum(wide(DOT, j, b)[64:128].astype(F32) * o, axis=0, keepdims=True)
+    def backward(level, j, weights, factor, delta, dot_t, rows):
+        p = weights[...] * factor
+        dp = nn(natural(level, j), dot_t)
+        ds = (p * (dp - delta)).astype(BF16)
+        return nn(ds, QM[j, rows]) + nn(p.astype(BF16), DOM[j, rows]), nn(KVT[level, j, 0:64], ds)
 
     def out_copy(i, src, row, n, k):
         return pltpu.make_async_remote_copy(
@@ -304,7 +278,7 @@
 
     parts = []
     for j in range(2):
-        parts += [(ROW_O[j], 64), (ROW_Q[j], 64), (ROW_KV[j], 128), (ROW_T8[j], 16)]
+        parts += [(ROW_Q[j][0], 64), (ROW_Q[j][1], 64), (ROW_KV[j], 128), (ROW_T8[j], 16)]
 
     def start_out(i):
         row, n = parts[i]
@@ -325,13 +299,6 @@
         og[:, row + 16:row + 64] = both[128:512].reshape(8, 48, 128)
         start_out(i)
 
-    def backward(level, j, b, width, qxt, dot_t, rows):
-        p = jnp.exp(nn(KX[level, j], qxt) - ST[0, j, b, :, :width])
-        dp = nn(natural(level, j), dot_t)
-        ds = (p * (dp - ST[1, j, b, :, :width])).astype(BF16)
-        ACC[level, j] += nn(ds, QM[j, rows]) + nn(p.astype(BF16), DOM[j, rows])
-        DQT[j, b, :, :width] += nn(KVT[level, j, 0:64], ds)
-
     def g32_copy(j, k):
         return pltpu.make_async_remote_copy(
             src_ref=g32.at[j, k], dst_ref=r32.at[j, 16 - k],
@@ -348,29 +315,6 @@
         return pltpu.make_async_remote_copy(
             src_ref=g2.at[j], dst_ref=r2.at[j], send_sem=l2_ss.at[2 + j], recv_sem=l2_rs.at[2 + j],
             device_id={"seq": pair}, device_id_type=MESH)
-
-    def backward_sparse(j):
-        backward(3, j, 0, 128, QXT32[j], DOT[j, 0], pl.ds(0, 128))
-        g32[j] = ACC[3, j].reshape(16, 2, 32, 128).astype(BF16)
-        for k in range(1, 16):
-            g32_copy(j, k).start()
-        backward(2, j, 0, 128, QXT[j, 0], DOT[j, 0], pl.ds(0, 128))
-        g8[j] = ACC[2, j].reshape(8, 128, 128).astype(BF16)
-        for k in range(1, 8):
-            g8_copy(j, k).start()
-
-    def backward_pair(j):
-        backward(1, j, 0, 512, wide(QXT, j, 0), wide(DOT, j, 0), pl.ds(0, 512))
-        g2[j] = ACC[1, j, 512:1024].reshape(8, 64, 128).astype(BF16)
-        g2_copy(j).start()
-
-    def backward_local(j):
-        def step(i, carry):
-            rows = pl.ds(pl.multiple_of(i * 512, 512), 512)
-            backward(0, j, i, 512, wide(QXT, j, i), wide(DOT, j, i), rows)
-            return carry
-
-        lax.fori_loop(0, 2, step, 0)
 
     put_row, put_col = iota((128, 32), 0), iota((128, 32), 1)
     put = (put_row == (put_col >> 2) * 16 + (put_col & 3)).astype(F32).astype(BF16)
@@ -409,46 +353,82 @@
     def prepare_local(j):
         prepare(0, j, lambda c: inbuf[2 * j, c])
 
-    def send_output(j):
-        send_rows(4 * j, OT[j, 0], OT[j, 1])
-
-    def send_queries(j):
-        send_rows(4 * j + 1, DQT[j, 0] * 0.125, DQT[j, 1] * 0.125)
+    def row_delta(j, part, o):
+        return jnp.sum(wide(DOT, j, part)[64:128].astype(F32) * o, axis=0, keepdims=True)
+
+    def attend_other(j):
+        prepare_queries(j, 1)
+        _, total, o = forward(0, j, wide(QXT, j, 1), W1)
+        factor = 1.0 / total
+        o = o * factor
+        acc, dq = backward(0, j, W1, factor, row_delta(j, 1, o), wide(DOT, j, 1), slice(512, 1024))
+        ACC[0, j] = acc if j == 0 else ACC[0, j] + acc
+        send_rows(4 * j + 1, dq * 0.125, o)
+
+    def attend_own(j, between):
+        m1, l1, o1 = forward(0, j, wide(QXT, j, 0), W1)
+        between()
+        l2_copy(j).wait()
+        prepare(1, j, lambda c: kv2[j, c // 4, pl.ds((c % 4) * 2, 2)].reshape(128, 128))
+        m2, l2, o2 = forward(1, j, wide(QXT, j, 0), W2)
+        for k in range(1, 8):
+            l8_copy(j, k).wait()
+        prepare(2, j, lambda c: kv8[j, c].reshape(128, 128))
+        m3, l3, o3 = forward(2, j, QXT[j, 0], W8)
+        for k in range(1, 16):
+            l32_copy(j, k).wait()
+        prepare(3, j, lambda c: kv32[j, pl.ds(2 * c, 2)].reshape(128, 128))
+        m4, l4, o4 = forward(3, j, QXT32[j], W32)
+
+        def on_first(x, f):
+            return jnp.concatenate([f(x[:, 0:128]), x[:, 128:512]], axis=1)
+
+        top = on_first(jnp.maximum(m1, m2), lambda x: jnp.maximum(x, jnp.maximum(m3, m4)))
+        e1, e2 = jnp.exp(m1 - top), jnp.exp(m2 - top)
+        e3, e4 = jnp.exp(m3 - top[:, 0:128]), jnp.exp(m4 - top[:, 0:128])
+        factor = 1.0 / on_first(l1 * e1 + l2 * e2, lambda x: x + l3 * e3 + l4 * e4)
+        o = on_first(o1 * e1 + o2 * e2, lambda x: x + o3 * e3 + o4 * e4) * factor
+        delta = row_delta(j, 0, o)
+        short = factor[:, 0:128], delta[:, 0:128]
+
+        ACC[1, j], dq2 = backward(1, j, W2, e2 * factor, delta, wide(DOT, j, 0), slice(0, 512))
+        g2[j] = ACC[1, j, 512:1024].reshape(8, 64, 128).astype(BF16)
+        g2_copy(j).start()
+        ACC[3, j], dq4 = backward(3, j, W32, e4 * short[0], short[1], DOT[j, 0], slice(0, 128))
+        g32[j] = ACC[3, j].reshape(16, 2, 32, 128).astype(BF16)
+        for k in range(1, 16):
+            g32_copy(j, k).start()
+        ACC[2, j], dq3 = backward(2, j, W8, e3 * short[0], short[1], DOT[j, 0], slice(0, 128))
+        g8[j] = ACC[2, j].reshape(8, 128, 128).astype(BF16)
+        for k in range(1, 8):
+            g8_copy(j, k).start()
+        acc, dq1 = backward(0, j, W1, e1 * factor, delta, wide(DOT, j, 0), slice(0, 512))
+        ACC[0, j] = acc if j == 1 else ACC[0, j] + acc
+        send_rows(4 * j, on_first(dq1 + dq2, lambda x: x + dq3 + dq4) * 0.125, o)
 
     wait_in(0)
-    start_keys(1)
     start_levels(0)
     prepare_local(0)
     wait_in(1)
-    start_in(3)
-    prepare_queries(0)
-    forward_first(0)
-    forward_rest(0)
-    send_output(0)
+    attend_other(0)
     wait_in(2)
     start_levels(1)
-    backward_pair(0)
-    backward_sparse(0)
     prepare_local(1)
-    backward_local(0)
-    send_queries(0)
     wait_in(3)
-    prepare_queries(1)
-    forward_first(1)
-    send_keys(0)
+    prepare_queries(0, 0)
+    attend_own(0, lambda: None)
+    wait_in(4)
+    prepare_queries(1, 0)
+    attend_own(1, lambda: send_keys(0))
     send_tiles(0)
-    forward_rest(1)
-    send_output(1)
-    backward_pair(1)
-    backward_sparse(1)
-    backward_local(1)
-    send_queries(1)
+    wait_in(5)
+    attend_other(1)
     send_keys(1)
     send_tiles(1)
 
-    for t in range(4):
+    for i in range(6):
         for k in range(1, NH):
-            in_copy(t, k).wait_send()
+            in_copy(i, k).wait_send()
     for j in range(2):
         for k in range(NH):
             zin_copy(j, k).wait_send()
@@ -461,15 +441,13 @@
 
 def restore_kernel(packed_ref, a_ref, q_ref, k_ref, v_ref):
     low = iota((128, 128), 1) < 64
-    low64 = iota((64, 128), 1) < 64
     for g in range(NH):
         rho = iota((NB, NB), 1)
         mat = (iota((NB, NB), 0) == token_of(rho >> 6, rho & 63, g)).astype(F32).astype(BF16)
         cols = []
-        for rows in (ROW_O, ROW_Q):
-            x, y = (packed_ref[g, row:row + 64].astype(F32) for row in rows)
-            odd = pltpu.roll(jnp.where(low64, y, x), 64, 1)
-            cols.append(jnp.concatenate([jnp.where(low64, x, y), odd], axis=0).astype(BF16))
+        for j in range(2):
+            both = [packed_ref[g, row:row + 64] for row in ROW_Q[j]]
+            cols.append(jnp.concatenate(both[::-1] if j else both, axis=0))
         for j in range(2):
             tile = sum(packed_ref[g, row:row + 16].astype(F32) for row in (ROW_KV[j], ROW_T8[j], ROW_TZ[j]))
             own = [tile.astype(BF16), packed_ref[g, ROW_KV[j] + 16:ROW_KV[j] + 64]]
@@ -477,11 +455,10 @@
             cols.append(jnp.concatenate(other + own if j else own + other, axis=0))
         res = nn(mat, jnp.concatenate(cols, axis=1))
         here = slice(g * 128, g * 128 + 128)
-        a_ref[:, here] = res[:, 0:128].astype(BF16)
-        q_ref[:, here] = res[:, 128:256].astype(BF16)
-        x, y = res[:, 256:384], res[:, 384:512]
-        k_ref[:, here] = jnp.where(low, x, pltpu.roll(y, 64, 1)).astype(BF16)
-        v_ref[:, here] = jnp.where(low, pltpu.roll(x, 64, 1), y).astype(BF16)
+        for first, second, at in ((q_ref, a_ref, 0), (k_ref, v_ref, 256)):
+            x, y = res[:, at:at + 128], res[:, at + 128:at + 256]
+            first[:, here] = jnp.where(low, x, pltpu.roll(y, 64, 1)).astype(BF16)
+            second[:, here] = jnp.where(low, pltpu.roll(x, 64, 1), y).astype(BF16)
 
 
 def body(queries, keys, values, grad_out, doc_ids):
@@ -502,15 +479,16 @@
             pltpu.VMEM((2, 16, 2, 32, 128), BF16),
             pltpu.VMEM((4, 2, 1024, 128), BF16),
             pltpu.VMEM((4, 2, 128, 1024), BF16),
-            pltpu.VMEM((1024, 128), BF16),
+            pltpu.VMEM((512, 128), BF16),
             pltpu.VMEM((2, 8, 128, 128), BF16),
             pltpu.VMEM((2, 128, 128), BF16),
             pltpu.VMEM((2, 1024, 128), BF16),
             pltpu.VMEM((2, 1024, 128), BF16),
             pltpu.VMEM((2, 8, 128, 128), BF16),
-            pltpu.VMEM((2, 2, 2, 1, 512), F32),
-            pltpu.VMEM((2, 2, 64, 512), F32),
-            pltpu.VMEM((2, 2, 64, 512), F32),
+            pltpu.VMEM((1024, 512), F32),
+            pltpu.VMEM((1024, 512), F32),
+            pltpu.VMEM((1024, 128), F32),
+            pltpu.VMEM((1024, 128), F32),
             pltpu.VMEM((4, 2, 1024, 128), F32),
             pltpu.VMEM((2, 8, 64, 128), BF16),
             pltpu.VMEM((2, 8, 64, 128), BF16),
@@ -519,7 +497,7 @@
             pltpu.VMEM((2, 16, 2, 32, 128), BF16),
             pltpu.VMEM((2, 16, 2, 32, 128), BF16),
             pltpu.VMEM((NH, ROWS, 128), BF16),
-            dma((5,)), dma((28,)), dma((28,)), dma((16,)), dma((16,)), dma((4,)),
+            dma((5,)), dma((42,)), dma((42,)), dma((16,)), dma((16,)), dma((6,)),
             dma((4,)), dma((4,)), dma((28,)), dma((28,)), dma((60,)), dma((60,)),
             dma((56,)), dma((56,)), dma((16,)), dma((16,)), dma((8,)),
         ],

time: 86 us -> 79.3 us (0.922)
  Pallas kernels: 84 us -> 77.3 us
    pallas_call x1, Pallas kernels: 82.5 us -> 75.7 us  [body(): pl.pallas_call(attend_kernel, out_shape=jax.ShapeDtypeStruct((NH, ROWS, 1...]
where the time goes in v2:
time: 79.3 us; the launch traced here: 79.2 us
  Pallas kernels  77.3 us (97%)
  local copies, waits for them, and re-layouts  1.26 us (2%)
    pallas_call x1, Pallas kernels, body(): pl.pallas_call(attend_kernel, out_shape=jax.ShapeDtypeStruct((NH, ROWS, 1...  75.7 us

profile of v2, /device:TPU:1, one launch (start us, length us, event | category | flops | bytes accessed | tf_op | source)
XLA Modules:
  0.0 79.2 jit_solution(5756326177881484462)
XLA Ops:
  0.6 75.7 %attend.1.packed_ref = bf16[8,576,128]{2,1,0:T(8,128)(2,1)} custom-call(bf16[128,1024]{1,0:T(8,128)(2,1)} %q_hbm.1, bf16[128,1024]{1,0:T(8,128)(2,1)} %k_hbm.1, bf16[128,1024]{1,0:T(8,128)(2,1)} %v_hbm.1, bf16[128,1024]{1,0:T(8,128)(2,1)} %do_hbm.1, s32[256,128]{1,0:T(8,128)} %bitcast.1), custom_call_target="tpu_custom_call" | custom-call | tf_op jit(solution)/shard_map/attend/pallas_call | solution.py:467
  76.4 0.0 copy-start
  76.4 1.3 %copy-done = bf16[8,576,128]{2,1,0:T(8,128)(2,1)S(1)} copy-done((bf16[8,576,128]{2,1,0:T(8,128)(2,1)S(1)}, bf16[8,576,128]{2,1,0:T(8,128)(2,1)}, u32[]{:S(2)}) %copy-start) | copy-done | bytes 1179672
  77.7 1.5 %restore.1 = (bf16[128,1024]{1,0:T(8,128)(2,1)}, bf16[128,1024]{1,0:T(8,128)(2,1)}, bf16[128,1024]{1,0:T(8,128)(2,1)}, bf16[128,1024]{1,0:T(8,128)(2,1)}) custom-call(bf16[8,576,128]{2,1,0:T(8,128)(2,1)S(1)} %copy-done), custom_call_target="tpu_custom_call" | custom-call | tf_op jit(solution)/shard_map/restore/pallas_call | solution.py:509
Async XLA Ops:
  76.4 1.3 %copy-start = (bf16[8,576,128]{2,1,0:T(8,128)(2,1)S(1)}, bf16[8,576,128]{2,1,0:T(8,128)(2,1)}, u32[]{:S(2)}) copy-start(bf16[8,576,128]{2,1,0:T(8,128)(2,1)} %attend.1.packed_ref) | copy-start | bytes 3538948

commit v3 on v2

--- a/solution.py
+++ b/solution.py
@@ -12,7 +12,7 @@
 NH = 8
 NB = 128
 MESH = pl.DeviceIdType.MESH
-ROW_Q, ROW_KV, ROW_T8, ROW_TZ, ROWS = ((0, 64), (128, 192)), (256, 384), (512, 528), (544, 560), 576
+ROW_Q, ROW_KV, ROW_TZ, ROWS = ((0, 64), (128, 192)), (256, 384), 512, 528
 
 
 def iota(shape, dim):
@@ -31,8 +31,8 @@
 def attend_kernel(
     q_hbm, k_hbm, v_hbm, do_hbm, docs_hbm, out_ref,
     q_ref, k_ref, v_ref, do_ref, docs_ref,
-    send, inbuf, zin, kv2, kv8, kv32, KX, KVT, QG, QXT, QXT32, QM, DOM, DOT,
-    W1, W2, W8, W32, ACC, g2, r2, g8, r8, g32, r32, og,
+    send, zsend, inbuf, zin, kv2, kv8, kv32, KX, KVT, QG, QXT, QXT32, QM, DOM, DOT,
+    WB, W1, W2, W8, W32, ACC, g2, r2, g8, r8, g32, r32, og,
     load_s, in_ss, in_rs, zin_ss, zin_rs, loc_s, l2_ss, l2_rs, l8_ss, l8_rs, l32_ss, l32_rs,
     out_ss, out_rs, tz_ss, tz_rs, out_loc,
 ):
@@ -52,6 +52,11 @@
     def head_peer(k):
         return (h + k) % NH
 
+    pairs = ((k_hbm, k_ref), (v_hbm, v_ref), (q_hbm, q_ref), (do_hbm, do_ref), (docs_hbm, docs_ref))
+    loads = [pltpu.make_async_copy(a, b, load_s.at[i]) for i, (a, b) in enumerate(pairs)]
+    for load in loads:
+        load.start()
+
     barrier = pltpu.get_barrier_semaphore()
     for k in range(1, NH):
         pl.semaphore_signal(barrier, inc=1, device_id={"head": head_peer(k)}, device_id_type=MESH)
@@ -60,11 +65,6 @@
     for k in range(NH):
         pl.semaphore_signal(barrier, inc=1, device_id={"seq": zpeer, "head": head_peer(k)}, device_id_type=MESH)
 
-    pairs = ((k_hbm, k_ref), (v_hbm, v_ref), (q_hbm, q_ref), (do_hbm, do_ref), (docs_hbm, docs_ref))
-    loads = [pltpu.make_async_copy(a, b, load_s.at[i]) for i, (a, b) in enumerate(pairs)]
-    for load in loads:
-        load.start()
-
     lane128 = iota((128, 128), 1)
     row128 = iota((128, 128), 0)
     low = lane128 < 64
@@ -75,12 +75,15 @@
             cols = slice(g * 128, g * 128 + 128)
             res = nn(mat, jnp.concatenate([a_ref[:, cols], b_ref[:, cols]], axis=1))
             a, b = res[:, 0:128], res[:, 128:256]
-            send[first, g] = jnp.where(low, a, pltpu.roll(b, 64, 1)).astype(BF16)
-            other = jnp.where(low, pltpu.roll(a, 64, 1), b).astype(BF16)
-            send[first + 2, g, 0:64] = other[64:128]
-            send[first + 2, g, 64:128] = other[0:64]
-
-    messages = ((0, 0, 128), (1, 64, 64), (2, 0, 128), (1, 0, 64), (3, 0, 64), (3, 64, 64))
+            one = jnp.where(low, a, pltpu.roll(b, 64, 1))
+            other = jnp.where(low, pltpu.roll(a, 64, 1), b)
+            send[first, g] = one.astype(BF16)
+            send[first + 2, g, 0:64] = other[64:128].astype(BF16)
+            send[first + 2, g, 64:128] = other[0:64].astype(BF16)
+            if first == 0:
+                zsend[g] = jnp.where(row128[0:16] < 4, one[0:16], pltpu.roll(other[64:80], 4, 0)).astype(BF16)
+
+    messages = ((0, 0, 128), (1, 0, 64), (1, 64, 64), (2, 0, 128), (3, 0, 64), (3, 64, 64))
 
     def in_copy(i, k):
         t, row, n = messages[i]
@@ -104,28 +107,23 @@
             in_copy(i, k).wait_recv()
         in_local(i).wait()
 
-    def zin_copy(j, k):
-        return pltpu.make_async_remote_copy(
-            src_ref=send.at[2 * j, head_peer(k), pl.ds(0, 16)], dst_ref=zin.at[j, h],
-            send_sem=zin_ss.at[8 * j + k], recv_sem=zin_rs.at[8 * j + k],
+    def zin_copy(k):
+        return pltpu.make_async_remote_copy(
+            src_ref=zsend.at[head_peer(k)], dst_ref=zin.at[h],
+            send_sem=zin_ss.at[k], recv_sem=zin_rs.at[k],
             device_id={"seq": zpeer, "head": head_peer(k)}, device_id_type=MESH)
-
-    def start_zin(j):
-        for k in range(NH):
-            zin_copy(j, k).start()
 
     loads[0].wait()
     loads[1].wait()
     permute_two(0, k_ref, v_ref)
     pl.semaphore_wait(barrier, 30)
-    start_zin(0)
+    for k in range(NH):
+        zin_copy(k).start()
     start_in(0)
     loads[2].wait()
     loads[3].wait()
     permute_two(1, q_ref, do_ref)
-    start_in(1)
-    start_zin(1)
-    for i in range(2, 6):
+    for i in range(1, 6):
         start_in(i)
     loads[4].wait()
 
@@ -199,31 +197,30 @@
             send_sem=l32_ss.at[15 * j + k - 1], recv_sem=l32_rs.at[15 * j + k - 1],
             device_id={"seq": plane_peer(k)}, device_id_type=MESH)
 
-    pick_row, pick_col = iota((32, 128), 0), iota((32, 128), 1)
-    pick = (pick_col == (pick_row >> 2) * 16 + (pick_row & 3)).astype(F32).astype(BF16)
+    def pick(j):
+        row, col = iota((32, 128), 0), iota((32, 128), 1)
+        return (col == (row >> 2) * 16 + (row & 3) + 4 * j).astype(F32).astype(BF16)
 
     def start_levels(j):
         l2_copy(j).start()
         for k in range(1, 8):
             l8_copy(j, k).start()
-        for k in range(NH):
-            zin_copy(j, k).wait_recv()
-        kv32[j, 0, 0] = nn(pick, inbuf[2 * j, :, 0:16].reshape(128, 128)).astype(BF16)
-        kv32[j, 0, 1] = nn(pick, zin[j].reshape(128, 128)).astype(BF16)
+        if j == 0:
+            for k in range(NH):
+                zin_copy(k).wait_recv()
+        kv32[j, 0, 0] = nn(pick(0), inbuf[2 * j, :, 0:16].reshape(128, 128)).astype(BF16)
+        kv32[j, 0, 1] = nn(pick(j), zin[...].reshape(128, 128)).astype(BF16)
         for k in range(1, 16):
             l32_copy(j, k).start()
         kv2[j, 0] = inbuf[2 * j, :, 0:64]
         kv8[j, 0] = inbuf[2 * j, :, 0:16]
 
     def prepare(level, j, load):
-        def chunk(c, carry):
-            rows = pl.ds(pl.multiple_of(c * 128, 128), 128)
+        for c in range(8):
+            rows = slice(c * 128, c * 128 + 128)
             kv = load(c).astype(F32)
             KX[level, j, rows] = jnp.where(low, kv, KX[level, j, rows].astype(F32)).astype(BF16)
             KVT[level, j, :, rows] = kv.T.astype(BF16)
-            return carry
-
-        lax.fori_loop(0, 8, chunk, 0)
 
     def natural(level, j):
         ref = (inbuf.at[2 * j], kv2.at[j], kv8.at[j], kv32.at[j])[level]
@@ -278,7 +275,7 @@
 
     parts = []
     for j in range(2):
-        parts += [(ROW_Q[j][0], 64), (ROW_Q[j][1], 64), (ROW_KV[j], 128), (ROW_T8[j], 16)]
+        parts += [(ROW_Q[j][0], 64), (ROW_Q[j][1], 64), (ROW_KV[j] + 16, 112), (ROW_KV[j], 16)]
 
     def start_out(i):
         row, n = parts[i]
@@ -286,10 +283,10 @@
             out_copy(i, og_part(row, n), row, n, k).start()
         out_local(i, og_part(row, n), row, n).start()
 
-    def tz_copy(j, k):
-        return pltpu.make_async_remote_copy(
-            src_ref=og.at[head_peer(k), pl.ds(ROW_TZ[j], 16)], dst_ref=out_ref.at[h, pl.ds(ROW_TZ[j], 16)],
-            send_sem=tz_ss.at[8 * j + k], recv_sem=tz_rs.at[8 * j + k],
+    def tz_copy(k):
+        return pltpu.make_async_remote_copy(
+            src_ref=og.at[head_peer(k), pl.ds(ROW_TZ, 16)], dst_ref=out_ref.at[h, pl.ds(ROW_TZ, 16)],
+            send_sem=tz_ss.at[k], recv_sem=tz_rs.at[k],
             device_id={"seq": zpeer, "head": head_peer(k)}, device_id_type=MESH)
 
     def send_rows(i, top, bottom):
@@ -316,39 +313,48 @@
             src_ref=g2.at[j], dst_ref=r2.at[j], send_sem=l2_ss.at[2 + j], recv_sem=l2_rs.at[2 + j],
             device_id={"seq": pair}, device_id_type=MESH)
 
-    put_row, put_col = iota((128, 32), 0), iota((128, 32), 1)
-    put = (put_row == (put_col >> 2) * 16 + (put_col & 3)).astype(F32).astype(BF16)
+    def put(j):
+        row, col = iota((128, 32), 0), iota((128, 32), 1)
+        return (row == (col >> 2) * 16 + (col & 3) + 4 * j).astype(F32).astype(BF16)
+
+    def spread(j, x):
+        hi = x.astype(BF16)
+        return nn(put(j), hi) + nn(put(j), (x - hi.astype(F32)).astype(BF16))
 
     def send_keys(j):
         g2_copy(j).wait()
         for b in range(8):
-            t2 = ACC[1, j, b * 64:b * 64 + 64] + r2[j, b].astype(F32)
-            own = ACC[0, j, b * 128:b * 128 + 128]
-            og[b, ROW_KV[j]:ROW_KV[j] + 64] = (own[0:64] + t2).astype(BF16)
-            og[b, ROW_KV[j] + 64:ROW_KV[j] + 128] = own[64:128].astype(BF16)
+            t2 = ACC[1, j, b * 64 + 16:b * 64 + 64] + r2[j, b, 16:64].astype(F32)
+            own = ACC[0, j, b * 128 + 16:b * 128 + 128]
+            og[b, ROW_KV[j] + 16:ROW_KV[j] + 64] = (own[0:48] + t2).astype(BF16)
+            og[b, ROW_KV[j] + 64:ROW_KV[j] + 128] = own[48:112].astype(BF16)
         start_out(4 * j + 2)
 
-    def spread(x):
-        hi = x.astype(BF16)
-        return nn(put, hi) + nn(put, (x - hi.astype(F32)).astype(BF16))
-
-    def send_tiles(j):
+    def sum_plane(j):
         for k in range(1, 16):
             g32_copy(j, k).wait()
-        mine, theirs = ACC[3, j, 0:32], ACC[3, j, 32:64]
+        total = ACC[3, j, 0:64]
         for m in range(1, 16):
-            mine += r32[j, m, 0].astype(F32)
-            theirs += r32[j, m, 1].astype(F32)
-        og[:, ROW_TZ[j]:ROW_TZ[j] + 16] = spread(theirs).astype(BF16).reshape(8, 16, 128)
-        for k in range(NH):
-            tz_copy(j, k).start()
+            total += r32[j, m].reshape(64, 128).astype(F32)
+        ACC[3, j, 0:64] = total
+
+    def send_tiles(j):
         for k in range(1, 8):
             g8_copy(j, k).wait()
-        t8 = ACC[2, j, 0:128] + spread(mine)
+        t8 = ACC[2, j, 0:128] + spread(0, ACC[3, j, 0:32])
         for m in range(1, 8):
             t8 += r8[j, m].astype(F32)
-        og[:, ROW_T8[j]:ROW_T8[j] + 16] = t8.astype(BF16).reshape(8, 16, 128)
+        for b in range(8):
+            t2 = ACC[1, j, b * 64:b * 64 + 16] + r2[j, b, 0:16].astype(F32)
+            own = ACC[0, j, b * 128:b * 128 + 16]
+            og[b, ROW_KV[j]:ROW_KV[j] + 16] = (own + t2 + t8[b * 16:b * 16 + 16]).astype(BF16)
         start_out(4 * j + 3)
+
+    def send_plane():
+        both = spread(0, ACC[3, 0, 32:64]) + spread(1, ACC[3, 1, 32:64])
+        og[:, ROW_TZ:ROW_TZ + 16] = both.astype(BF16).reshape(8, 16, 128)
+        for k in range(NH):
+            tz_copy(k).start()
 
     def prepare_local(j):
         prepare(0, j, lambda c: inbuf[2 * j, c])
@@ -358,18 +364,18 @@
 
     def attend_other(j):
         prepare_queries(j, 1)
-        _, total, o = forward(0, j, wide(QXT, j, 1), W1)
+        _, total, o = forward(0, j, wide(QXT, j, 1), WB)
         factor = 1.0 / total
         o = o * factor
-        acc, dq = backward(0, j, W1, factor, row_delta(j, 1, o), wide(DOT, j, 1), slice(512, 1024))
-        ACC[0, j] = acc if j == 0 else ACC[0, j] + acc
+        acc, dq = backward(0, j, WB, factor, row_delta(j, 1, o), wide(DOT, j, 1), slice(512, 1024))
+        ACC[0, j] = acc
         send_rows(4 * j + 1, dq * 0.125, o)
 
-    def attend_own(j, between):
+    def attend_own(j, before, after):
         m1, l1, o1 = forward(0, j, wide(QXT, j, 0), W1)
-        between()
+        before()
         l2_copy(j).wait()
-        prepare(1, j, lambda c: kv2[j, c // 4, pl.ds((c % 4) * 2, 2)].reshape(128, 128))
+        prepare(1, j, lambda c: kv2[j, c // 4, c % 4 * 2:c % 4 * 2 + 2].reshape(128, 128))
         m2, l2, o2 = forward(1, j, wide(QXT, j, 0), W2)
         for k in range(1, 8):
             l8_copy(j, k).wait()
@@ -377,7 +383,7 @@
         m3, l3, o3 = forward(2, j, QXT[j, 0], W8)
         for k in range(1, 16):
             l32_copy(j, k).wait()
-        prepare(3, j, lambda c: kv32[j, pl.ds(2 * c, 2)].reshape(128, 128))
+        prepare(3, j, lambda c: kv32[j, 2 * c:2 * c + 2].reshape(128, 128))
         m4, l4, o4 = forward(3, j, QXT32[j], W32)
 
         def on_first(x, f):
@@ -394,6 +400,7 @@
         ACC[1, j], dq2 = backward(1, j, W2, e2 * factor, delta, wide(DOT, j, 0), slice(0, 512))
         g2[j] = ACC[1, j, 512:1024].reshape(8, 64, 128).astype(BF16)
         g2_copy(j).start()
+        after()
         ACC[3, j], dq4 = backward(3, j, W32, e4 * short[0], short[1], DOT[j, 0], slice(0, 128))
         g32[j] = ACC[3, j].reshape(16, 2, 32, 128).astype(BF16)
         for k in range(1, 16):
@@ -403,36 +410,45 @@
         for k in range(1, 8):
             g8_copy(j, k).start()
         acc, dq1 = backward(0, j, W1, e1 * factor, delta, wide(DOT, j, 0), slice(0, 512))
-        ACC[0, j] = acc if j == 1 else ACC[0, j] + acc
+        ACC[0, j] += acc
         send_rows(4 * j, on_first(dq1 + dq2, lambda x: x + dq3 + dq4) * 0.125, o)
+
+    def other_first():
+        wait_in(2)
+        attend_other(0)
+
+    def other_second():
+        send_keys(0)
+        wait_in(5)
+        attend_other(1)
+
+    def next_levels():
+        wait_in(3)
+        start_levels(1)
 
     wait_in(0)
     start_levels(0)
     prepare_local(0)
     wait_in(1)
-    attend_other(0)
-    wait_in(2)
-    start_levels(1)
+    prepare_queries(0, 0)
+    attend_own(0, other_first, next_levels)
     prepare_local(1)
-    wait_in(3)
-    prepare_queries(0, 0)
-    attend_own(0, lambda: None)
     wait_in(4)
     prepare_queries(1, 0)
-    attend_own(1, lambda: send_keys(0))
+    attend_own(1, other_second, lambda: None)
+    sum_plane(0)
     send_tiles(0)
-    wait_in(5)
-    attend_other(1)
     send_keys(1)
+    sum_plane(1)
+    send_plane()
     send_tiles(1)
 
     for i in range(6):
         for k in range(1, NH):
             in_copy(i, k).wait_send()
-    for j in range(2):
-        for k in range(NH):
-            zin_copy(j, k).wait_send()
-            tz_copy(j, k).wait()
+    for k in range(NH):
+        zin_copy(k).wait_send()
+        tz_copy(k).wait()
     for i, (row, n) in enumerate(parts):
         for k in range(1, NH):
             out_copy(i, og_part(row, n), row, n, k).wait()
@@ -441,6 +457,7 @@
 
 def restore_kernel(packed_ref, a_ref, q_ref, k_ref, v_ref):
     low = iota((128, 128), 1) < 64
+    first4 = iota((16, 128), 0) < 4
     for g in range(NH):
         rho = iota((NB, NB), 1)
         mat = (iota((NB, NB), 0) == token_of(rho >> 6, rho & 63, g)).astype(F32).astype(BF16)
@@ -449,7 +466,9 @@
             both = [packed_ref[g, row:row + 64] for row in ROW_Q[j]]
             cols.append(jnp.concatenate(both[::-1] if j else both, axis=0))
         for j in range(2):
-            tile = sum(packed_ref[g, row:row + 16].astype(F32) for row in (ROW_KV[j], ROW_T8[j], ROW_TZ[j]))
+            plane = packed_ref[g, ROW_TZ:ROW_TZ + 16].astype(F32)
+            plane = jnp.where(first4, pltpu.roll(plane, 12, 0) if j else plane, 0.0)
+            tile = packed_ref[g, ROW_KV[j]:ROW_KV[j] + 16].astype(F32) + plane
             own = [tile.astype(BF16), packed_ref[g, ROW_KV[j] + 16:ROW_KV[j] + 64]]
             other = [packed_ref[g, ROW_KV[j] + 64:ROW_KV[j] + 128]]
             cols.append(jnp.concatenate(other + own if j else own + other, axis=0))
@@ -472,8 +491,9 @@
         scratch_shapes=[pltpu.VMEM(queries.shape, BF16)] * 4 + [
             pltpu.VMEM((256, 128), I32),
             pltpu.VMEM((4, NH, NB, 128), BF16),
+            pltpu.VMEM((NH, 16, 128), BF16),
             pltpu.VMEM((4, NH, NB, 128), BF16),
-            pltpu.VMEM((2, 8, 16, 128), BF16),
+            pltpu.VMEM((NH, 16, 128), BF16),
             pltpu.VMEM((2, 2, 8, 64, 128), BF16),
             pltpu.VMEM((2, 8, 8, 16, 128), BF16),
             pltpu.VMEM((2, 16, 2, 32, 128), BF16),
@@ -487,6 +507,7 @@
             pltpu.VMEM((2, 8, 128, 128), BF16),
             pltpu.VMEM((1024, 512), F32),
             pltpu.VMEM((1024, 512), F32),
+            pltpu.VMEM((1024, 512), F32),
             pltpu.VMEM((1024, 128), F32),
             pltpu.VMEM((1024, 128), F32),
             pltpu.VMEM((4, 2, 1024, 128), F32),
@@ -497,9 +518,9 @@
             pltpu.VMEM((2, 16, 2, 32, 128), BF16),
             pltpu.VMEM((2, 16, 2, 32, 128), BF16),
             pltpu.VMEM((NH, ROWS, 128), BF16),
-            dma((5,)), dma((42,)), dma((42,)), dma((16,)), dma((16,)), dma((6,)),
+            dma((5,)), dma((42,)), dma((42,)), dma((8,)), dma((8,)), dma((6,)),
             dma((4,)), dma((4,)), dma((28,)), dma((28,)), dma((60,)), dma((60,)),
-            dma((56,)), dma((56,)), dma((16,)), dma((16,)), dma((8,)),
+            dma((56,)), dma((56,)), dma((8,)), dma((8,)), dma((8,)),
         ],
         compiler_params=pltpu.CompilerParams(
             collective_id=0, has_side_effects=True, vmem_limit_bytes=56 * 1024 * 1024),

time: 79.3 us -> 74.6 us (0.941)
  Pallas kernels: 77.3 us -> 72.6 us
    pallas_call x1, Pallas kernels: 75.7 us -> 71 us  [body(): pl.pallas_call(attend_kernel, out_shape=jax.ShapeDtypeStruct((NH, ROWS, 1...]
where the time goes in v3:
time: 74.6 us; the launch traced here: 74.4 us
  Pallas kernels  72.6 us (97%)
  local copies, waits for them, and re-layouts  1.23 us (2%)
    pallas_call x1, Pallas kernels, body(): pl.pallas_call(attend_kernel, out_shape=jax.ShapeDtypeStruct((NH, ROWS, 1...  71 us
    pallas_call x1, Pallas kernels, body(): pl.pallas_call(restore_kernel, out_shape=(shape, shape, shape, shape), in...  1.53 us

profile of v3, /device:TPU:1, one launch (start us, length us, event | category | flops | bytes accessed | tf_op | source)
XLA Modules:
  0.0 74.4 jit_solution(16524480853463065130)
XLA Ops:
  0.6 71.0 %attend.1.packed_ref = bf16[8,528,128]{2,1,0:T(8,128)(2,1)} custom-call(bf16[128,1024]{1,0:T(8,128)(2,1)} %q_hbm.1, bf16[128,1024]{1,0:T(8,128)(2,1)} %k_hbm.1, bf16[128,1024]{1,0:T(8,128)(2,1)} %v_hbm.1, bf16[128,1024]{1,0:T(8,128)(2,1)} %do_hbm.1, s32[256,128]{1,0:T(8,128)} %bitcast.1), custom_call_target="tpu_custom_call" | custom-call | tf_op jit(solution)/shard_map/attend/pallas_call | solution.py:486
  71.7 0.0 copy-start
  71.7 1.2 %copy-done = bf16[8,528,128]{2,1,0:T(8,128)(2,1)S(1)} copy-done((bf16[8,528,128]{2,1,0:T(8,128)(2,1)S(1)}, bf16[8,528,128]{2,1,0:T(8,128)(2,1)}, u32[]{:S(2)}) %copy-start) | copy-done | bytes 1081368
  72.9 1.5 %restore.1 = (bf16[128,1024]{1,0:T(8,128)(2,1)}, bf16[128,1024]{1,0:T(8,128)(2,1)}, bf16[128,1024]{1,0:T(8,128)(2,1)}, bf16[128,1024]{1,0:T(8,128)(2,1)}) custom-call(bf16[8,528,128]{2,1,0:T(8,128)(2,1)S(1)} %copy-done), custom_call_target="tpu_custom_call" | custom-call | tf_op jit(solution)/shard_map/restore/pallas_call | solution.py:530
Async XLA Ops:
  71.7 1.2 %copy-start = (bf16[8,528,128]{2,1,0:T(8,128)(2,1)S(1)}, bf16[8,528,128]{2,1,0:T(8,128)(2,1)}, u32[]{:S(2)}) copy-start(bf16[8,528,128]{2,1,0:T(8,128)(2,1)} %attend.1.packed_ref) | copy-start | bytes 3244036

commit v4 on v3

--- a/solution.py
+++ b/solution.py
@@ -83,7 +83,8 @@
             if first == 0:
                 zsend[g] = jnp.where(row128[0:16] < 4, one[0:16], pltpu.roll(other[64:80], 4, 0)).astype(BF16)
 
-    messages = ((0, 0, 128), (1, 0, 64), (1, 64, 64), (2, 0, 128), (3, 0, 64), (3, 64, 64))
+    messages = tuple((t, row, 64) for t, row in (
+        (0, 0), (2, 0), (0, 64), (1, 64), (1, 0), (2, 64), (3, 0), (3, 64)))
 
     def in_copy(i, k):
         t, row, n = messages[i]
@@ -119,11 +120,12 @@
     pl.semaphore_wait(barrier, 30)
     for k in range(NH):
         zin_copy(k).start()
-    start_in(0)
+    for i in range(3):
+        start_in(i)
     loads[2].wait()
     loads[3].wait()
     permute_two(1, q_ref, do_ref)
-    for i in range(1, 6):
+    for i in range(3, 8):
         start_in(i)
     loads[4].wait()
 
@@ -275,7 +277,8 @@
 
     parts = []
     for j in range(2):
-        parts += [(ROW_Q[j][0], 64), (ROW_Q[j][1], 64), (ROW_KV[j] + 16, 112), (ROW_KV[j], 16)]
+        parts += [(ROW_Q[j][0], 64), (ROW_Q[j][1], 64), (ROW_KV[j] + 16, 48), (ROW_KV[j], 16),
+                  (ROW_KV[j] + 64, 64)]
 
     def start_out(i):
         row, n = parts[i]
@@ -325,10 +328,14 @@
         g2_copy(j).wait()
         for b in range(8):
             t2 = ACC[1, j, b * 64 + 16:b * 64 + 64] + r2[j, b, 16:64].astype(F32)
-            own = ACC[0, j, b * 128 + 16:b * 128 + 128]
-            og[b, ROW_KV[j] + 16:ROW_KV[j] + 64] = (own[0:48] + t2).astype(BF16)
-            og[b, ROW_KV[j] + 64:ROW_KV[j] + 128] = own[48:112].astype(BF16)
-        start_out(4 * j + 2)
+            own = ACC[0, j, b * 128 + 16:b * 128 + 64]
+            og[b, ROW_KV[j] + 16:ROW_KV[j] + 64] = (own + t2).astype(BF16)
+        start_out(5 * j + 2)
+
+    def send_other_keys(j):
+        for b in range(8):
+            og[b, ROW_KV[j] + 64:ROW_KV[j] + 128] = ACC[0, j, b * 128 + 64:b * 128 + 128].astype(BF16)
+        start_out(5 * j + 4)
 
     def sum_plane(j):
         for k in range(1, 16):
@@ -348,7 +355,7 @@
             t2 = ACC[1, j, b * 64:b * 64 + 16] + r2[j, b, 0:16].astype(F32)
             own = ACC[0, j, b * 128:b * 128 + 16]
             og[b, ROW_KV[j]:ROW_KV[j] + 16] = (own + t2 + t8[b * 16:b * 16 + 16]).astype(BF16)
-        start_out(4 * j + 3)
+        start_out(5 * j + 3)
 
     def send_plane():
         both = spread(0, ACC[3, 0, 32:64]) + spread(1, ACC[3, 1, 32:64])
@@ -368,10 +375,10 @@
         factor = 1.0 / total
         o = o * factor
         acc, dq = backward(0, j, WB, factor, row_delta(j, 1, o), wide(DOT, j, 1), slice(512, 1024))
-        ACC[0, j] = acc
-        send_rows(4 * j + 1, dq * 0.125, o)
-
-    def attend_own(j, before, after):
+        ACC[0, j] = acc if j == 0 else ACC[0, j] + acc
+        send_rows(5 * j + 1, dq * 0.125, o)
+
+    def attend_own(j, before):
         m1, l1, o1 = forward(0, j, wide(QXT, j, 0), W1)
         before()
         l2_copy(j).wait()
@@ -400,7 +407,6 @@
         ACC[1, j], dq2 = backward(1, j, W2, e2 * factor, delta, wide(DOT, j, 0), slice(0, 512))
         g2[j] = ACC[1, j, 512:1024].reshape(8, 64, 128).astype(BF16)
         g2_copy(j).start()
-        after()
         ACC[3, j], dq4 = backward(3, j, W32, e4 * short[0], short[1], DOT[j, 0], slice(0, 128))
         g32[j] = ACC[3, j].reshape(16, 2, 32, 128).astype(BF16)
         for k in range(1, 16):
@@ -410,32 +416,29 @@
         for k in range(1, 8):
             g8_copy(j, k).start()
         acc, dq1 = backward(0, j, W1, e1 * factor, delta, wide(DOT, j, 0), slice(0, 512))
-        ACC[0, j] += acc
-        send_rows(4 * j, on_first(dq1 + dq2, lambda x: x + dq3 + dq4) * 0.125, o)
-
-    def other_first():
-        wait_in(2)
-        attend_other(0)
-
-    def other_second():
-        send_keys(0)
-        wait_in(5)
-        attend_other(1)
-
-    def next_levels():
-        wait_in(3)
-        start_levels(1)
+        ACC[0, j] = acc if j == 1 else ACC[0, j] + acc
+        send_rows(5 * j, on_first(dq1 + dq2, lambda x: x + dq3 + dq4) * 0.125, o)
 
     wait_in(0)
     start_levels(0)
+    wait_in(1)
+    start_levels(1)
+    wait_in(2)
     prepare_local(0)
-    wait_in(1)
+    wait_in(3)
+    attend_other(0)
+    wait_in(4)
     prepare_queries(0, 0)
-    attend_own(0, other_first, next_levels)
+    attend_own(0, lambda: None)
+    send_other_keys(0)
+    wait_in(5)
     prepare_local(1)
-    wait_in(4)
+    wait_in(6)
     prepare_queries(1, 0)
-    attend_own(1, other_second, lambda: None)
+    attend_own(1, lambda: send_keys(0))
+    wait_in(7)
+    attend_other(1)
+    send_other_keys(1)
     sum_plane(0)
     send_tiles(0)
     send_keys(1)
@@ -443,7 +446,7 @@
     send_plane()
     send_tiles(1)
 
-    for i in range(6):
+    for i in range(8):
         for k in range(1, NH):
             in_copy(i, k).wait_send()
     for k in range(NH):
@@ -518,9 +521,9 @@
             pltpu.VMEM((2, 16, 2, 32, 128), BF16),
             pltpu.VMEM((2, 16, 2, 32, 128), BF16),
             pltpu.VMEM((NH, ROWS, 128), BF16),
-            dma((5,)), dma((42,)), dma((42,)), dma((8,)), dma((8,)), dma((6,)),
+            dma((5,)), dma((56,)), dma((56,)), dma((8,)), dma((8,)), dma((8,)),
             dma((4,)), dma((4,)), dma((28,)), dma((28,)), dma((60,)), dma((60,)),
-            dma((56,)), dma((56,)), dma((8,)), dma((8,)), dma((8,)),
+            dma((70,)), dma((70,)), dma((8,)), dma((8,)), dma((10,)),
         ],
         compiler_params=pltpu.CompilerParams(
             collective_id=0, has_side_effects=True, vmem_limit_bytes=56 * 1024 * 1024),

time: 74.6 us -> 71 us (0.952)
  Pallas kernels: 72.6 us -> 68.9 us
    pallas_call x1, Pallas kernels: 71 us -> 67.4 us  [body(): pl.pallas_call(attend_kernel, out_shape=jax.ShapeDtypeStruct((NH, ROWS, 1...]
where the time goes in v4:
time: 71 us; the launch traced here: 70.8 us
  Pallas kernels  68.9 us (97%)
  local copies, waits for them, and re-layouts  1.23 us (2%)
    pallas_call x1, Pallas kernels, body(): pl.pallas_call(attend_kernel, out_shape=jax.ShapeDtypeStruct((NH, ROWS, 1...  67.4 us
    pallas_call x1, Pallas kernels, body(): pl.pallas_call(restore_kernel, out_shape=(shape, shape, shape, shape), in...  1.53 us

profile of v4, /device:TPU:1, one launch (start us, length us, event | category | flops | bytes accessed | tf_op | source)
XLA Modules:
  0.0 70.8 jit_solution(465670656735808031)
XLA Ops:
  0.6 67.4 %attend.1.packed_ref = bf16[8,528,128]{2,1,0:T(8,128)(2,1)} custom-call(bf16[128,1024]{1,0:T(8,128)(2,1)} %q_hbm.1, bf16[128,1024]{1,0:T(8,128)(2,1)} %k_hbm.1, bf16[128,1024]{1,0:T(8,128)(2,1)} %v_hbm.1, bf16[128,1024]{1,0:T(8,128)(2,1)} %do_hbm.1, s32[256,128]{1,0:T(8,128)} %bitcast.1), custom_call_target="tpu_custom_call" | custom-call | tf_op jit(solution)/shard_map/attend/pallas_call | solution.py:489
  68.1 0.0 copy-start
  68.1 1.2 %copy-done = bf16[8,528,128]{2,1,0:T(8,128)(2,1)S(1)} copy-done((bf16[8,528,128]{2,1,0:T(8,128)(2,1)S(1)}, bf16[8,528,128]{2,1,0:T(8,128)(2,1)}, u32[]{:S(2)}) %copy-start) | copy-done | bytes 1081368
  69.3 1.5 %restore.1 = (bf16[128,1024]{1,0:T(8,128)(2,1)}, bf16[128,1024]{1,0:T(8,128)(2,1)}, bf16[128,1024]{1,0:T(8,128)(2,1)}, bf16[128,1024]{1,0:T(8,128)(2,1)}) custom-call(bf16[8,528,128]{2,1,0:T(8,128)(2,1)S(1)} %copy-done), custom_call_target="tpu_custom_call" | custom-call | tf_op jit(solution)/shard_map/restore/pallas_call | solution.py:533
Async XLA Ops:
  68.1 1.2 %copy-start = (bf16[8,528,128]{2,1,0:T(8,128)(2,1)S(1)}, bf16[8,528,128]{2,1,0:T(8,128)(2,1)}, u32[]{:S(2)}) copy-start(bf16[8,528,128]{2,1,0:T(8,128)(2,1)} %attend.1.packed_ref) | copy-start | bytes 3244036

commit v5 on v4

--- a/solution.py
+++ b/solution.py
@@ -436,11 +436,11 @@
     wait_in(6)
     prepare_queries(1, 0)
     attend_own(1, lambda: send_keys(0))
+    sum_plane(0)
+    send_tiles(0)
     wait_in(7)
     attend_other(1)
     send_other_keys(1)
-    sum_plane(0)
-    send_tiles(0)
     send_keys(1)
     sum_plane(1)
     send_plane()
@@ -488,9 +488,9 @@
     dma = pltpu.SemaphoreType.DMA
     packed = pl.pallas_call(
         attend_kernel,
-        out_shape=jax.ShapeDtypeStruct((NH, ROWS, 128), BF16),
+        out_shape=pltpu.VMEM((NH, ROWS, 128), BF16),
         in_specs=[pl.BlockSpec(memory_space=pl.ANY)] * 5,
-        out_specs=pl.BlockSpec(memory_space=pl.ANY),
+        out_specs=vmem,
         scratch_shapes=[pltpu.VMEM(queries.shape, BF16)] * 4 + [
             pltpu.VMEM((256, 128), I32),
             pltpu.VMEM((4, NH, NB, 128), BF16),

time: 71 us -> 69.8 us (0.983)
  local copies, waits for them, and re-layouts: 1.23 us -> 0 us
    unnamed x2 -> x0, local copies, waits for them, and re-layouts: 1.23 us -> none
where the time goes in v5:
time: 69.8 us; the launch traced here: 69.7 us
  Pallas kernels  69 us (99%)
    pallas_call x1, Pallas kernels, body(): pl.pallas_call(attend_kernel, out_shape=pltpu.VMEM((NH, ROWS, 128), BF16)...  67.5 us
    pallas_call x1, Pallas kernels, body(): pl.pallas_call(restore_kernel, out_shape=(shape, shape, shape, shape), in...  1.53 us

profile of v5, /device:TPU:1, one launch (start us, length us, event | category | flops | bytes accessed | tf_op | source)
XLA Modules:
  0.0 69.7 jit_solution(8806795171539149082)
XLA Ops:
  0.6 67.5 %attend.1.packed_ref = bf16[8,528,128]{2,1,0:T(8,128)(2,1)S(1)} custom-call(bf16[128,1024]{1,0:T(8,128)(2,1)} %q_hbm.1, bf16[128,1024]{1,0:T(8,128)(2,1)} %k_hbm.1, bf16[128,1024]{1,0:T(8,128)(2,1)} %v_hbm.1, bf16[128,1024]{1,0:T(8,128)(2,1)} %do_hbm.1, s32[256,128]{1,0:T(8,128)} %bitcast.1), custom_call_target="tpu_custom_call" | custom-call | tf_op jit(solution)/shard_map/attend/pallas_call | solution.py:489
  68.1 1.5 %restore.1 = (bf16[128,1024]{1,0:T(8,128)(2,1)}, bf16[128,1024]{1,0:T(8,128)(2,1)}, bf16[128,1024]{1,0:T(8,128)(2,1)}, bf16[128,1024]{1,0:T(8,128)(2,1)}) custom-call(bf16[8,528,128]{2,1,0:T(8,128)(2,1)S(1)} %attend.1.packed_ref), custom_call_target="tpu_custom_call" | custom-call | tf_op jit(solution)/shard_map/restore/pallas_call | solution.py:533

commit v6 on v5

--- a/solution.py
+++ b/solution.py
@@ -378,9 +378,8 @@
         ACC[0, j] = acc if j == 0 else ACC[0, j] + acc
         send_rows(5 * j + 1, dq * 0.125, o)
 
-    def attend_own(j, before):
+    def attend_own(j, meanwhile):
         m1, l1, o1 = forward(0, j, wide(QXT, j, 0), W1)
-        before()
         l2_copy(j).wait()
         prepare(1, j, lambda c: kv2[j, c // 4, c % 4 * 2:c % 4 * 2 + 2].reshape(128, 128))
         m2, l2, o2 = forward(1, j, wide(QXT, j, 0), W2)
@@ -415,6 +414,7 @@
         g8[j] = ACC[2, j].reshape(8, 128, 128).astype(BF16)
         for k in range(1, 8):
             g8_copy(j, k).start()
+        meanwhile()
         acc, dq1 = backward(0, j, W1, e1 * factor, delta, wide(DOT, j, 0), slice(0, 512))
         ACC[0, j] = acc if j == 1 else ACC[0, j] + acc
         send_rows(5 * j, on_first(dq1 + dq2, lambda x: x + dq3 + dq4) * 0.125, o)

time: 69.8 us -> 69.8 us (level)
  no operation moved by 1% of the time
where the time goes in v6:
time: 69.8 us; the launch traced here: 69.7 us
  Pallas kernels  69.1 us (99%)
    pallas_call x1, Pallas kernels, body(): pl.pallas_call(attend_kernel, out_shape=pltpu.VMEM((NH, ROWS, 128), BF16)...  67.5 us
    pallas_call x1, Pallas kernels, body(): pl.pallas_call(restore_kernel, out_shape=(shape, shape, shape, shape), in...  1.53 us

profile of v6, /device:TPU:1, one launch (start us, length us, event | category | flops | bytes accessed | tf_op | source)
XLA Modules:
  0.0 69.7 jit_solution(2560760801245703786)
XLA Ops:
  0.6 67.5 %attend.1.packed_ref = bf16[8,528,128]{2,1,0:T(8,128)(2,1)S(1)} custom-call(bf16[128,1024]{1,0:T(8,128)(2,1)} %q_hbm.1, bf16[128,1024]{1,0:T(8,128)(2,1)} %k_hbm.1, bf16[128,1024]{1,0:T(8,128)(2,1)} %v_hbm.1, bf16[128,1024]{1,0:T(8,128)(2,1)} %do_hbm.1, s32[256,128]{1,0:T(8,128)} %bitcast.1), custom_call_target="tpu_custom_call" | custom-call | tf_op jit(solution)/shard_map/attend/pallas_call | solution.py:489
  68.2 1.5 %restore.1 = (bf16[128,1024]{1,0:T(8,128)(2,1)}, bf16[128,1024]{1,0:T(8,128)(2,1)}, bf16[128,1024]{1,0:T(8,128)(2,1)}, bf16[128,1024]{1,0:T(8,128)(2,1)}) custom-call(bf16[8,528,128]{2,1,0:T(8,128)(2,1)S(1)} %attend.1.packed_ref), custom_call_target="tpu_custom_call" | custom-call | tf_op jit(solution)/shard_map/restore/pallas_call | solution.py:533
